TPU v7x, 32 devices: a whole 2x2x4 slice. The times are simulated.
32 devices in a mesh: ctx: 8 (over z, y), ch: 4 (over x, core).
Axes of the slice: x: 2, y: 2, z: 4, core: 2. Of those that a mesh axis runs over, the one named last changes fastest.
Arguments:
- outer_gate: bfloat16 [2048, 4096], P('ctx', 'ch'), may hold values from -6 to 6
- inner_gate: bfloat16 [2048, 4096], P('ctx', 'ch'), may hold values from -6 to 6
- values_in: bfloat16 [2048, 4096], P('ctx', 'ch'), may hold values from -6 to 6
- filters: float32 [2048, 4096], P('ctx', 'ch'), as said below
- skip_gain: float32 [4096], P('ch'), may hold values from 0.5 to 1.5
- w_out: bfloat16 [4096, 4096], P('ch', 'ctx'), may hold values from -0.125 to 0.125
Outputs:
- mixed: bfloat16 [2048, 4096], P('ctx', 'ch')
Inputs may be any that keep to these rules, and one draw needn't show every extreme that they name: `filters`: finite values.
All inputs are finite; a program needn't handle non-finite values.
Results may differ from a plain program's by a relative error of at most 0.022.
Values may be sent and summed in bfloat16 or wider, within the bound.
No kernel may reach another device: no remote copies, remote signals or barrier semaphores. Data moves between devices by JAX's collectives and lax.ppermute only.
A program may use at most 128 MiB of HBM per device.

v0:
```python
import math

import jax
import jax.numpy as jnp
from jax import lax
from jax.sharding import PartitionSpec as P


def from_behind(block, axis, distance):
    devices = range(lax.axis_size(axis))
    route = [(i - distance, i) for i in devices if i - distance in devices]
    return lax.ppermute(block, axis, route)


def forward_table(block):
    length = 2 * block
    rows = jnp.arange(block, dtype=jnp.int32)[:, None]
    freqs = jnp.arange(length, dtype=jnp.int32)[None, :]
    angles = 2.0 * math.pi / length * (rows * freqs % length).astype(jnp.float32)
    return jnp.concatenate([jnp.cos(angles), -jnp.sin(angles)], axis=1)


def inverse_table(block):
    length = 2 * block
    freqs = jnp.arange(length, dtype=jnp.int32)[:, None]
    places = jnp.arange(length, dtype=jnp.int32)[None, :]
    angles = 2.0 * math.pi / length * (freqs * places % length).astype(jnp.float32)
    return jnp.concatenate([jnp.cos(angles), -jnp.sin(angles)], axis=0) / length


def split_table(table):
    upper_part = table.astype(jnp.bfloat16)
    lower_part = (table - upper_part.astype(jnp.float32)).astype(jnp.bfloat16)
    return (upper_part, lower_part)


def spectrum(series, table):
    return lax.dot_general(
        series,
        table,
        (((0,), (0,)), ((), ())),
        precision=lax.Precision.HIGH,
        preferred_element_type=jnp.float32,
    )


def narrow_spectrum(series, tables):
    dims = (((0,), (0,)), ((), ()))
    first = lax.dot_general(series, tables[0], dims, preferred_element_type=jnp.float32)
    return first + lax.dot_general(series, tables[1], dims, preferred_element_type=jnp.float32)


def complex_product(left, right):
    half = left.shape[-1] // 2
    left_re, left_im = (left[..., :half], left[..., half:])
    right_re, right_im = (right[..., :half], right[..., half:])
    return jnp.concatenate(
        [left_re * right_re - left_im * right_im, left_re * right_im + left_im * right_re], axis=-1
    )


def per_device(outer_gate, inner_gate, values_in, filters, skip_gain, w_out):
    block = outer_gate.shape[0]
    chans = outer_gate.shape[1]
    length = 2 * block
    gated = (inner_gate.astype(jnp.float32) * values_in.astype(jnp.float32)).astype(jnp.bfloat16)
    forward = forward_table(block)
    forward_parts = split_table(forward)
    inverse = inverse_table(block)
    whole_filter = lax.all_gather(filters.astype(jnp.bfloat16), "ctx", axis=0, tiled=True).astype(
        filters.dtype
    )
    mine = lax.axis_index("ctx")
    empty = jnp.zeros((chans, 2 * length), jnp.float32)
    piece = lax.all_gather(gated[None], "ctx", axis=0, tiled=True)

    def one_block(k, acc):
        distance = mine - k

        def live(inner):
            lag_rows = lax.dynamic_slice_in_dim(
                whole_filter, jnp.maximum(distance, 0) * block, block, 0
            )
            source = lax.dynamic_index_in_dim(piece, k, 0, keepdims=False)
            return inner + complex_product(
                narrow_spectrum(source, forward_parts), spectrum(lag_rows, forward)
            )

        return lax.cond(distance >= 0, live, lambda inner: inner, acc)

    summed = lax.fori_loop(0, piece.shape[0], one_block, empty)
    wave = lax.dot_general(
        inverse,
        summed,
        (((0,), (1,)), ((), ())),
        precision=lax.Precision.HIGH,
        preferred_element_type=jnp.float32,
    )
    carried = from_behind(wave[block:].astype(jnp.bfloat16), "ctx", 1).astype(jnp.float32)
    conv = wave[:block] + carried
    mix_in = (
        outer_gate.astype(jnp.float32) * (conv + skip_gain[None, :] * gated.astype(jnp.float32))
    ).astype(jnp.bfloat16)
    partial_rows = jnp.dot(
        mix_in, lax.all_gather(w_out, "ctx", axis=1, tiled=True), preferred_element_type=jnp.float32
    )
    return lax.psum_scatter(
        partial_rows.astype(jnp.bfloat16), "ch", scatter_dimension=1, tiled=True
    )


def solution(mesh):
    placed = (
        P("ctx", "ch"),
        P("ctx", "ch"),
        P("ctx", "ch"),
        P("ctx", "ch"),
        P("ch"),
        P("ch", "ctx"),
    )
    return jax.shard_map(
        per_device, mesh=mesh, in_specs=placed, out_specs=P("ctx", "ch"), check_vma=False
    )
```

profile of v0, /device:TPU:2, one launch (start us, length us, event | category | flops | bytes accessed | tf_op | source)
XLA Modules:
  0.0 350.6 jit_solution(15630659213541671427)
XLA Ops:
  6.5 2.1 convert_element_type.66
  8.8 2.2 multiply_convert_fusion
  11.0 0.7 all-gather.7.cloned.1.call-update
  11.8 2.1 sine_negate_fusion.1
  13.9 0.2 pad_maximum_fusion
  14.1 5.3 %sine_negate_fusion = (f32[512,512]{1,0:T(8,128)S(1)}, f32[512,512]{1,0:T(8,128)}) fusion(), kind=kLoop, calls=%fused_computation.34 | loop fusion | flops 3932160 | bytes 2097152 | tf_op jit(solution)/shard_map/neg | solution.py:28
  19.3 64.8 %all-gather.5.cloned.1.call-done = bf16[2048,1024]{1,0:T(8,128)(2,1)} async-done(((bf16[256,1024]{1,0:T(8,128)(2,1)}), bf16[2048,1024]{1,0:T(8,128)(2,1)}) %all-gather.5.cloned.1.call-update) | async-done | bytes 4194320 | tf_op jit(solution)/shard_map/all_gather | solution.py:70
  84.2 6.5 %convert_element_type.67 = f32[2048,1024]{1,0:T(8,128)} convert(bf16[2048,1024]{1,0:T(8,128)(2,1)} %all-gather.5.cloned.1.call-done) | non-fusion elementwise | flops 2097152 | bytes 12582912 | tf_op jit(solution)/shard_map/convert_element_type | solution.py:70
  90.6 67.4 %all-gather.9.cloned.1.call-done = bf16[2048,1024]{1,0:T(8,128)(2,1)} async-done(((bf16[256,1024]{1,0:T(8,128)(2,1)}), bf16[2048,1024]{1,0:T(8,128)(2,1)}) %all-gather.9.cloned.1.call-update) | async-done | bytes 4194320 | tf_op jit(solution)/shard_map/all_gather | solution.py:75
  158.0 2.5 broadcast_in_dim.4
  160.5 15.5 %while.16 = (s32[]{:T(128)}, f32[1024,1024]{0,1:T(8,128)}, s32[]{:T(128)}, bf16[8,256,1024]{2,1,0:T(8,128)(2,1)}, bf16[256,1024]{1,0:T(8,128)(2,1)S(1)}, /*index...) while((s32[]{:T(128)}, f32[1024,1024]{0,1:T(8,128)}, ...), condition=%wide.region_3.4_spmd, body=%wide.region_0.3_spmd.sunk | while | flops 2690646016 | bytes 62914888 | solution.py:91
  160.5 15.5 %conditional.2 = (f32[1024,1024]{0,1:T(8,128)}) conditional(s32[]{:T(128)} %convert_element_type.104, f32[1024,1024]{0,1:T(8,128)} %get-tuple-element.261, (s32[]{:T(128)}, bf16[8,256,1024]{2,1,0:T(8,128)(2,1)}, bf16[256,1024]{1,0:T(8,128)(2,1)S(1)}, bf16[256,1024]{1,0:T(8,128)(2,1)S(1)}, s32[]{:T(128)}, /*index=5*/f32[2048,1024]{1,0:T(8,128)}, ...), branch_computations={%region_1.1_spmd, %region_2.2_spmd} | conditional | flops 2690646016 | bytes 62914700 | solution.py:89
  160.5 1.8 fusion.3
  162.3 3.8 %convolution_add_fusion = f32[1024,1024]{0,1:T(8,128)} fusion(f32[1024,1024]{0,1:T(8,128)S(1)} %fusion.3, bf16[256,1024]{1,0:T(8,128)(2,1)S(1)} %get-tuple-element.162, bf16[8,256,1024]{2,1,0:T(8,128)(2,1)} %get-tuple-element.159, s32[]{:T(128)S(6)} %select_n.18), kind=kOutput, calls=%fused_computation.1 | convolution fusion | flops 537919488 | bytes 9437188 | tf_op jit(solution)/shard_map/while/body/eval_jaxpr/cond/branch_1_fun/dot_general | solution.py:50
  166.1 3.4 fusion
  169.5 1.0 multiply_subtract_fusion
  170.5 5.5 %maximum_add_fusion = f32[1024,1024]{0,1:T(8,128)} fusion(f32[1024,1024]{0,1:T(8,128)} %get-tuple-element.158, f32[1024,512]{0,1:T(8,128)S(1)} %get-tuple-element.194, f32[1024,512]{0,1:T(8,128)S(1)} %get-tuple-element.193), kind=kLoop, calls=%fused_computation | loop fusion | flops 2097152 | bytes 12582912 | tf_op jit(solution)/shard_map/while/body/eval_jaxpr/cond/branch_1_fun/add | solution.py:85
  176.0 5.7 %fusion.10 = f32[512,1024]{1,0:T(8,128)S(1)} fusion(f32[1024,1024]{0,1:T(8,128)} %get-tuple-element.176, f32[512,512]{1,0:T(8,128)S(1)} %get-tuple-element.199, f32[512,512]{1,0:T(8,128)} %get-tuple-element.200), kind=kOutput, calls=%fused_computation.16 | convolution fusion | flops 3222274048 | bytes 8388608 | tf_op jit(solution)/shard_map/dot_general | solution.py:92
  181.8 0.1 slice.44
  181.9 17.9 %collective-permute-start = (bf16[256,1024]{1,0:T(8,128)(2,1)S(1)}, bf16[256,1024]{1,0:T(8,128)(2,1)S(1)}, u32[]{:S(2)}, u32[]{:S(2)}) collective-permute-start(bf16[256,1024]{1,0:T(8,128)(2,1)S(1)} %slice.44), channel_id=1, source_target_pairs={{0,4},{4,8},{8,12},{12,16},{16,20},{20,24},{24,28},{1,5},{5,9},{9,... | collective-permute-start | bytes 1572872 | tf_op jit(solution)/shard_map/ppermute | solution.py:12
  199.8 10.0 %collective-permute-done = bf16[256,1024]{1,0:T(8,128)(2,1)S(1)} collective-permute-done((bf16[256,1024]{1,0:T(8,128)(2,1)S(1)}, bf16[256,1024]{1,0:T(8,128)(2,1)S(1)}, u32[]{:S(2)}, u32[]{:S(2)}) %collective-permute-start) | collective-permute-done | bytes 524320 | tf_op jit(solution)/shard_map/ppermute | solution.py:12
  209.8 83.3 %all-gather.7.cloned.1.call-done = bf16[1024,4096]{1,0:T(8,128)(2,1)} async-done(((bf16[1024,512]{1,0:T(8,128)(2,1)}), bf16[1024,4096]{1,0:T(8,128)(2,1)}) %all-gather.7.cloned.1.call-update) | async-done | bytes 8388624 | tf_op jit(solution)/shard_map/all_gather | solution.py:105
  293.0 7.5 %convolution_convert_fusion = bf16[256,4096]{1,0:T(8,128)(2,1)} fusion(bf16[1024,4096]{1,0:T(8,128)(2,1)} %all-gather.7.cloned.1.call-done, f32[512,1024]{1,0:T(8,128)S(1)} %fusion.10, bf16[256,1024]{1,0:T(8,128)(2,1)} %multiply_convert_fusion, bf16[256,1024]{1,0:T(8,128)(2,1)S(1)} %collective-permute-done, bf16[256,1024]{1,0:T(8,128)(2,1)} %param.10, ...), kind=kOutput, calls=%fused_computation.14 | convolution fusion | flops 2150629376 | bytes 13111296 | tf_op jit(solution)/shard_map/dot_general | solution.py:104
  300.5 43.5 %reduce-scatter.2.cloned.1.call-done = bf16[256,1024]{1,0:T(8,128)(2,1)} async-done(((bf16[256,4096]{1,0:T(8,128)(2,1)}), bf16[256,1024]{1,0:T(8,128)(2,1)}) %reduce-scatter.2.cloned.1.call-update) | async-done | bytes 524304 | tf_op jit(solution)/shard_map/reduce_scatter | solution.py:107
  (19 shorter events, 0.2 us)
Async XLA Ops:
  6.5 77.6 %all-gather.5.cloned.1.call-start = ((), (), s32[]{:S(2)}) async-start(), calls=%async_computation.1 | async-start | bytes 4718592 | tf_op jit(solution)/shard_map/all_gather | solution.py:70
  8.7 149.3 %all-gather.9.cloned.1.call-start = ((), (), s32[]{:S(2)}) async-start(), calls=%async_computation.4 | async-start | bytes 4718592 | tf_op jit(solution)/shard_map/all_gather | solution.py:75
  11.0 282.1 %all-gather.7.cloned.1.call-start = ((), (), s32[]{:S(2)}) async-start(), calls=%async_computation.2 | async-start | bytes 9437184 | tf_op jit(solution)/shard_map/all_gather | solution.py:105
  11.7 332.3 %reduce-scatter.2.cloned.1.call-start = ((), (), s32[]{:S(2)}) async-start(), calls=%async_computation.3 | async-start | bytes 2621440 | tf_op jit(solution)/shard_map/reduce_scatter | solution.py:107
  166.1 3.4 copy-start
  176.0 117.0 %copy-start.1 = (f32[1024]{0:T(1024)S(1)}, f32[1024]{0:T(1024)}, u32[]{:S(2)}) copy-start(f32[1024]{0:T(1024)} %param.14) | copy-start | bytes 12292
  181.9 27.9 %collective-permute-start = (bf16[256,1024]{1,0:T(8,128)(2,1)S(1)}, bf16[256,1024]{1,0:T(8,128)(2,1)S(1)}, u32[]{:S(2)}, u32[]{:S(2)}) collective-permute-start(bf16[256,1024]{1,0:T(8,128)(2,1)S(1)} %slice.44), channel_id=1, source_target_pairs={{0,4},{4,8},{8,12},{12,16},{16,20},{20,24},{24,28},{1,5},{5,9},{9,... | collective-permute-start | bytes 1572872 | tf_op jit(solution)/shard_map/ppermute | solution.py:12
Sparse Core Ops, SparseCore 0:
  9.5 74.6 all-gather.4
  86.3 71.6 all-gather.8
  160.0 132.9 all-gather.6
  300.7 43.3 reduce-scatter.1
where the time goes:
time: 354 us; the launch traced here: 351 us
  waiting for transfers between devices  270 us (76%)
  other arithmetic  24.9 us (7%)
  matrix products  22.2 us (6%)
  starting transfers between devices  18.1 us (5%)
  between operations  13.2 us (4%)
    all_gather x1, waiting for transfers between devices, per_device(): lax.all_gather(w_out, 'ctx', axis=1, tiled=True)  83.3 us
    all_gather x1, waiting for transfers between devices, per_device(): piece = lax.all_gather(gated[None], 'ctx', axis=0, tiled=True)  67.4 us
    all_gather x1, waiting for transfers between devices, per_device(): lax.all_gather(filters.astype(jnp.bfloat16), 'ctx', axis=0, tiled=True)  64.8 us
    reduce_scatter x1, waiting for transfers between devices, per_device(): lax.psum_scatter(partial_rows.astype(jnp.bfloat16), 'ch', scatter_dimensi...  43.5 us
    ppermute x1, starting transfers between devices, from_behind(): return lax.ppermute(block, axis, route)  17.9 us
    ppermute x1, waiting for transfers between devices, from_behind(): return lax.ppermute(block, axis, route)  9.96 us
    dot_general x1, matrix products, per_device(): jnp.dot(mix_in, lax.all_gather(w_out, 'ctx', axis=1, tiled=True), preferr...  7.49 us
  transfers between devices with their start and end apart: 5, of which 5 were waited for; matrix products, arithmetic and copies ran while one was open for 11% of the time, Pallas kernels for 0%

commit v1 on v0

v1 whole, which is shorter than its diff:
```python
import functools
import math

import jax
import jax.numpy as jnp
import numpy as np
from jax import lax
from jax.experimental import pallas as pl
from jax.experimental.pallas import tpu as pltpu
from jax.sharding import PartitionSpec as P


def tables(block):
    freqs = np.arange(block, dtype=np.float64)[:, None] + 0.5
    window = np.arange(-block, block, dtype=np.float64)[None, :]
    angles = math.pi / block * freqs * window
    forward = np.concatenate([np.cos(angles), -np.sin(angles)], axis=0)
    places = angles[:, block:].T
    inverse = np.concatenate([np.cos(places), -np.sin(places)], axis=1) / block
    return forward.astype(jnp.bfloat16), inverse.astype(jnp.bfloat16)


def conv_kernel(gf_ref, outer_ref, skip_ref, fwd_ref, inv_ref, mix_ref, xs, gs, ys):
    n, _, block, chans = gf_ref.shape
    f32 = jnp.float32
    for k in range(n):
        xs[k] = jnp.dot(fwd_ref[:, block:], gf_ref[k, 0], preferred_element_type=f32)
        lag = jnp.dot(fwd_ref[:, block:], gf_ref[k, 1], preferred_element_type=f32)
        if k:
            lag += jnp.dot(fwd_ref[:, :block], gf_ref[k - 1, 1], preferred_element_type=f32)
        gs[k] = lag

    step = 8

    @pl.loop(0, block // step)
    def _(c):
        re = pl.ds(pl.multiple_of(c * step, step), step)
        im = pl.ds(pl.multiple_of(block + c * step, step), step)
        xr = [xs[k, re, :] for k in range(n)]
        xi = [xs[k, im, :] for k in range(n)]
        gr = [gs[k, re, :] for k in range(n)]
        gi = [gs[k, im, :] for k in range(n)]
        xt = [a + b for a, b in zip(xr, xi)]
        gt = [a + b for a, b in zip(gr, gi)]
        for i in range(n):
            one = xr[0] * gr[i]
            two = xi[0] * gi[i]
            three = xt[0] * gt[i]
            for k in range(1, i + 1):
                one += xr[k] * gr[i - k]
                two += xi[k] * gi[i - k]
                three += xt[k] * gt[i - k]
            ys[i, re, :] = one - two
            ys[i, im, :] = three - (one + two)

    for i in range(n):
        conv = jnp.dot(inv_ref[...], ys[i].astype(jnp.bfloat16), preferred_element_type=f32)
        mix = outer_ref[i].astype(f32) * (conv + skip_ref[...] * gf_ref[i, 0].astype(f32))
        mix_ref[i * block : (i + 1) * block, :] = mix.astype(jnp.bfloat16)


def convolve(pair, outer, skip):
    n, _, block, chans = pair.shape
    forward, inverse = tables(block)
    return pl.pallas_call(
        conv_kernel,
        out_shape=jax.ShapeDtypeStruct((n * block, chans), jnp.bfloat16),
        scratch_shapes=[pltpu.VMEM((n, 2 * block, chans), jnp.float32)] * 3,
        compiler_params=pltpu.CompilerParams(vmem_limit_bytes=40 * 2**20),
        name="convolve",
    )(pair, outer, skip, jnp.asarray(forward), jnp.asarray(inverse))


def per_device(outer_gate, inner_gate, values_in, filters, skip_gain, w_out):
    n, m = lax.axis_size("ctx"), lax.axis_size("ch")
    j, k = lax.axis_index("ctx"), lax.axis_index("ch")
    block, wide = outer_gate.shape
    chans = wide // n
    gated = (inner_gate.astype(jnp.float32) * values_in.astype(jnp.float32)).astype(jnp.bfloat16)

    def cut(rows):
        return rows.reshape(block, n, chans).transpose(1, 0, 2)

    pair = jnp.stack([cut(gated), cut(filters.astype(jnp.bfloat16))], axis=1)
    pair = lax.all_to_all(pair, "ctx", 0, 0)
    outer = lax.all_to_all(cut(outer_gate), "ctx", 0, 0)
    skip = lax.dynamic_slice_in_dim(skip_gain, j * chans, chans, 0)[None, :]
    mix = convolve(pair, outer, skip)
    whole = lax.all_gather(mix, "ctx", axis=1, tiled=True)
    part = jnp.dot(whole, w_out, preferred_element_type=jnp.float32).astype(jnp.bfloat16)
    bit = 1
    groups = part.reshape((m, -1, part.shape[1]))
    while bit < m:
        mine = (k // bit) % 2
        split = groups.reshape((groups.shape[0] // 2, 2) + groups.shape[1:])
        keep = lax.dynamic_index_in_dim(split, mine, 1, keepdims=False)
        give = lax.dynamic_index_in_dim(split, 1 - mine, 1, keepdims=False)
        got = lax.ppermute(give, "ch", [(d, d ^ bit) for d in range(m)])
        groups = (keep.astype(jnp.float32) + got.astype(jnp.float32)).astype(jnp.bfloat16)
        bit *= 2
    q = n // m
    rows = groups.reshape(q, block, part.shape[1])
    found = []
    for e in range(q):
        sent = lax.dynamic_index_in_dim(rows, (j + e) % q, 0, keepdims=False)
        route = []
        for a in range(n):
            for b in range(m):
                route.append((a * m + b, (q * b + (a + e) % q) * m + a // q))
        found.append(lax.ppermute(sent, ("ctx", "ch"), route))
    columns = [
        lax.select_n((j - h) % q, *found) if q > 1 else found[0] for h in range(q)
    ]
    return jnp.concatenate(columns, axis=1)


def solution(mesh):
    placed = (
        P("ctx", "ch"),
        P("ctx", "ch"),
        P("ctx", "ch"),
        P("ctx", "ch"),
        P("ch"),
        P("ch", "ctx"),
    )
    return jax.shard_map(
        per_device, mesh=mesh, in_specs=placed, out_specs=P("ctx", "ch"), check_vma=False
    )
```

time: 354 us -> 198 us (0.56)
  waiting for transfers between devices: 270 us -> 145 us
  other arithmetic: 24.9 us -> 4.88 us
  matrix products: 22.2 us -> 4.52 us
  local copies, waits for them, and re-layouts: 2.59 us -> 7.62 us
  Pallas kernels: 0 us -> 4.66 us
    all_gather x3 -> x1, waiting for transfers between devices: 215 us -> 74.2 us  [per_device(): whole = lax.all_gather(mix, 'ctx', axis=1, tiled=True)]
    reduce_scatter x1 -> x0, waiting for transfers between devices: 43.5 us -> none  [per_device(): lax.psum_scatter(partial_rows.astype(jnp.bfloat16), 'ch', scatter_dimensi...]
    all_to_all x0 -> x2, waiting for transfers between devices: none -> 34.3 us  [the longest x1 25.1 us: per_device(): pair = lax.all_to_all(pair, 'ctx', 0, 0)]
    ppermute x1 -> x4, waiting for transfers between devices: 9.96 us -> 36.5 us  [the longest x2 20.5 us: per_device(): found.append(lax.ppermute(sent, ('ctx', 'ch'), route))]
    dot_general x5 -> x1, matrix products: 22.2 us -> 4.52 us  [per_device(): jnp.dot(whole, w_out, preferred_element_type=jnp.float32)]
    ppermute x1 -> x4, starting transfers between devices: 17.9 us -> 7.37 us  [the longest x2 6.68 us: per_device(): found.append(lax.ppermute(sent, ('ctx', 'ch'), route))]
    all_to_all x0 -> x2, starting transfers between devices: none -> 9.47 us  [the longest x1 5.83 us: per_device(): outer = lax.all_to_all(cut(outer_gate), 'ctx', 0, 0)]
    neg x2 -> x0, other arithmetic: 7.35 us -> none  [the longest x1 5.28 us: inverse_table(): return jnp.concatenate([jnp.cos(angles), -jnp.sin(angles)], axis=0) / length]
  transfers between devices with their start and end apart: 5 -> 7, of which waited for: 5 -> 7; matrix products, arithmetic and copies ran while one was open for 11% -> 3% of each run, Pallas kernels for 0% -> 0%
where the time goes in v1:
time: 198 us; the launch traced here: 197 us
  waiting for transfers between devices  145 us (73%)
  starting transfers between devices  16.9 us (9%)
  between operations  13.6 us (7%)
  local copies, waits for them, and re-layouts  7.62 us (4%)
  other arithmetic  4.88 us (2%)
  Pallas kernels  4.66 us (2%)
  matrix products  4.52 us (2%)
    all_gather x1, waiting for transfers between devices, per_device(): whole = lax.all_gather(mix, 'ctx', axis=1, tiled=True)  74.2 us
    all_to_all x1, waiting for transfers between devices, per_device(): pair = lax.all_to_all(pair, 'ctx', 0, 0)  25.1 us
    ppermute x2, waiting for transfers between devices, per_device(): found.append(lax.ppermute(sent, ('ctx', 'ch'), route))  20.5 us
    ppermute x2, waiting for transfers between devices, per_device(): got = lax.ppermute(give, 'ch', [(d, d ^ bit) for d in range(m)])  16 us
    all_to_all x1, waiting for transfers between devices, per_device(): outer = lax.all_to_all(cut(outer_gate), 'ctx', 0, 0)  9.16 us
    ppermute x2, starting transfers between devices, per_device(): found.append(lax.ppermute(sent, ('ctx', 'ch'), route))  6.68 us
    all_to_all x1, starting transfers between devices, per_device(): outer = lax.all_to_all(cut(outer_gate), 'ctx', 0, 0)  5.83 us
    pallas_call x1, Pallas kernels, convolve(): pl.pallas_call(conv_kernel, out_shape=jax.ShapeDtypeStruct((n * block, ch...  4.66 us
  transfers between devices with their start and end apart: 7, of which 7 were waited for; matrix products, arithmetic and copies ran while one was open for 3% of the time, Pallas kernels for 0%

profile of v1, /device:TPU:2, one launch (start us, length us, event | category | flops | bytes accessed | tf_op | source)
XLA Modules:
  0.0 197.1 jit_solution(17454793964216557105)
XLA Ops:
  6.5 1.4 copy.14
  7.9 1.0 copy.15
  9.0 5.8 %all-to-all-start.1 = ((bf16[8,256,128]{2,1,0:T(8,128)(2,1)}), bf16[8,256,128]{2,1,0:T(8,128)(2,1)S(1)}, u32[]{:S(2)}, u32[]{:S(2)}) async-start(bf16[8,256,128]{2,1,0:T(8,128)(2,1)} %bitcast.7), calls=%async_computation.1 | async-start | bytes 1048576 | tf_op jit(solution)/shard_map/all_to_all | solution.py:86
  15.0 1.0 copy.13
  16.0 1.2 copy.10
  17.6 0.3 copy.11
  17.9 2.2 %pad_maximum_fusion = bf16[8,2,256,128]{3,2,1,0:T(8,128)(2,1)} fusion(bf16[8,1,256,128]{3,2,1,0:T(8,128)(2,1)} %bitcast.31, bf16[8,1,256,128]{3,2,1,0:T(8,128)(2,1)S(1)} %bitcast.32), kind=kLoop, calls=%fused_computation.3 | loop fusion | flops 524288 | bytes 2097152 | tf_op jit(solution)/shard_map/stack | solution.py:84
  20.1 9.2 %all-to-all-done.1.outer_ref = bf16[8,256,128]{2,1,0:T(8,128)(2,1)S(1)} async-done(((bf16[8,256,128]{2,1,0:T(8,128)(2,1)}), bf16[8,256,128]{2,1,0:T(8,128)(2,1)S(1)}, u32[]{:S(2)}, u32[]{:S(2)}) %all-to-all-start.1) | async-done | bytes 524320 | tf_op jit(solution)/shard_map/all_to_all | solution.py:86
  29.3 3.6 %all-to-all-start = ((bf16[8,2,256,128]{3,2,1,0:T(8,128)(2,1)}), bf16[8,2,256,128]{3,2,1,0:T(8,128)(2,1)S(1)}, u32[]{:S(2)}, u32[]{:S(2)}) async-start(bf16[8,2,256,128]{3,2,1,0:T(8,128)(2,1)} %pad_maximum_fusion), calls=%async_computation | async-start | bytes 2097152 | tf_op jit(solution)/shard_map/all_to_all | solution.py:85
  33.0 0.8 dynamic-slice_bitcast_fusion.3.skip_ref
  33.7 25.1 %all-to-all-done.gf_ref = bf16[8,2,256,128]{3,2,1,0:T(8,128)(2,1)S(1)} async-done(((bf16[8,2,256,128]{3,2,1,0:T(8,128)(2,1)}), bf16[8,2,256,128]{3,2,1,0:T(8,128)(2,1)S(1)}, u32[]{:S(2)}, u32[]{:S(2)}) %all-to-all-start) | async-done | bytes 1048608 | tf_op jit(solution)/shard_map/all_to_all | solution.py:85
  58.9 4.7 %convolve.1 = bf16[2048,128]{1,0:T(8,128)(2,1)} custom-call(bf16[8,2,256,128]{3,2,1,0:T(8,128)(2,1)S(1)} %all-to-all-done.gf_ref, bf16[8,256,128]{2,1,0:T(8,128)(2,1)S(1)} %all-to-all-done.1.outer_ref, f32[1,128]{1,0:T(1,128)S(1)} %dynamic-slice_bitcast_fusion.3.skip_ref, bf16[512,512]{1,0:T(8,128)(2,1)S(1)} %copy-done.1, bf16[256,512]{1,0:T(8,128)(2,1)S(1)} %copy-done.2), custom_call_target="tpu_custom_call" | custom-call | tf_op jit(solution)/shard_map/convolve/pallas_call | solution.py:65
  63.6 74.2 %all-gather.2.cloned.1.call-done = bf16[2048,1024]{1,0:T(8,128)(2,1)} async-done(((bf16[2048,128]{1,0:T(8,128)(2,1)}), bf16[2048,1024]{1,0:T(8,128)(2,1)}) %all-gather.2.cloned.1.call-update) | async-done | bytes 4194320 | tf_op jit(solution)/shard_map/all_gather | solution.py:89
  137.8 4.5 %convolution_convert_fusion = bf16[2048,512]{1,0:T(8,128)(2,1)S(1)} fusion(bf16[2048,1024]{1,0:T(8,128)(2,1)} %all-gather.2.cloned.1.call-done, bf16[1024,512]{1,0:T(8,128)(2,1)S(1)} %copy-done), kind=kOutput, calls=%fused_computation | convolution fusion | flops 2148532224 | bytes 7340032 | tf_op jit(solution)/shard_map/dot_general | solution.py:90
  142.3 1.3 copy-done.3
  143.8 2.6 %collective-permute-done = bf16[2,512,512]{2,1,0:T(8,128)(2,1)S(1)} collective-permute-done((bf16[2,512,512]{2,1,0:T(8,128)(2,1)S(1)}, bf16[2,512,512]{2,1,0:T(8,128)(2,1)S(1)}, u32[]{:S(2)}, u32[]{:S(2)}) %collective-permute-start) | collective-permute-done | bytes 1048608 | tf_op jit(solution)/shard_map/ppermute | solution.py:98
  146.4 1.5 fusion
  148.0 0.6 collective-permute-start.1
  148.6 13.4 %collective-permute-done.1 = bf16[1,512,512]{2,1,0:T(8,128)(2,1)S(1)} collective-permute-done((bf16[1,512,512]{2,1,0:T(8,128)(2,1)S(1)}, bf16[1,512,512]{2,1,0:T(8,128)(2,1)S(1)}, u32[]{:S(2)}, u32[]{:S(2)}) %collective-permute-start.1) | collective-permute-done | bytes 524320 | tf_op jit(solution)/shard_map/ppermute | solution.py:98
  162.2 3.4 %collective-permute-start.2 = (bf16[256,512]{1,0:T(8,128)(2,1)S(1)}, bf16[256,512]{1,0:T(8,128)(2,1)S(1)}, u32[]{:S(2)}, u32[]{:S(2)}) collective-permute-start(bf16[256,512]{1,0:T(8,128)(2,1)S(1)} %get-tuple-element.8), channel_id=1, source_target_pairs={{0,0},{1,8},{2,16},{3,24},{4,4},{5,12},{6,20},{7,28},{8,1},{9,9},{... | collective-permute-start | bytes 786440 | tf_op jit(solution)/shard_map/ppermute | solution.py:110
  165.6 3.3 %collective-permute-start.3 = (bf16[256,512]{1,0:T(8,128)(2,1)S(1)}, bf16[256,512]{1,0:T(8,128)(2,1)S(1)}, u32[]{:S(2)}, u32[]{:S(2)}) collective-permute-start(bf16[256,512]{1,0:T(8,128)(2,1)S(1)} %get-tuple-element.7), channel_id=1, source_target_pairs={{0,4},{1,12},{2,20},{3,28},{4,0},{5,8},{6,16},{7,24},{8,5},{9,13},... | collective-permute-start | bytes 786440 | tf_op jit(solution)/shard_map/ppermute | solution.py:110
  168.9 14.9 %collective-permute-done.2 = bf16[256,512]{1,0:T(8,128)(2,1)S(1)} collective-permute-done((bf16[256,512]{1,0:T(8,128)(2,1)S(1)}, bf16[256,512]{1,0:T(8,128)(2,1)S(1)}, u32[]{:S(2)}, u32[]{:S(2)}) %collective-permute-start.2) | collective-permute-done | bytes 262176 | tf_op jit(solution)/shard_map/ppermute | solution.py:110
  183.8 5.6 %collective-permute-done.3 = bf16[256,512]{1,0:T(8,128)(2,1)S(1)} collective-permute-done((bf16[256,512]{1,0:T(8,128)(2,1)S(1)}, bf16[256,512]{1,0:T(8,128)(2,1)S(1)}, u32[]{:S(2)}, u32[]{:S(2)}) %collective-permute-start.3) | collective-permute-done | bytes 262176 | tf_op jit(solution)/shard_map/ppermute | solution.py:110
  189.4 0.9 pad_maximum_fusion.1
  (22 shorter events, 1.0 us)
Async XLA Ops:
  6.5 131.2 %copy-start = (bf16[1024,512]{1,0:T(8,128)(2,1)S(1)}, bf16[1024,512]{1,0:T(8,128)(2,1)}, u32[]{:S(2)}) copy-start(bf16[1024,512]{1,0:T(8,128)(2,1)} %param.13) | copy-start | bytes 3145732
  6.5 8.3 %copy-start.4 = (f32[256,1024]{1,0:T(8,128)S(1)}, f32[256,1024]{1,0:T(8,128)}, u32[]{:S(2)}) copy-start(f32[256,1024]{1,0:T(8,128)} %param.11) | copy-start | bytes 3145732
  9.0 20.3 %all-to-all-start.1 = ((bf16[8,256,128]{2,1,0:T(8,128)(2,1)}), bf16[8,256,128]{2,1,0:T(8,128)(2,1)S(1)}, u32[]{:S(2)}, u32[]{:S(2)}) async-start(bf16[8,256,128]{2,1,0:T(8,128)(2,1)} %bitcast.7), calls=%async_computation.1 | async-start | bytes 1048576 | tf_op jit(solution)/shard_map/all_to_all | solution.py:86
  15.0 2.3 %copy-start.5 = (bf16[256,1024]{1,0:T(8,128)(2,1)S(1)}, bf16[256,1024]{1,0:T(8,128)(2,1)}, u32[]{:S(2)}) copy-start(bf16[256,1024]{1,0:T(8,128)(2,1)} %param.9) | copy-start | bytes 1572868
  17.9 41.0 %copy-start.1 = (bf16[512,512]{1,0:T(8,128)(2,1)S(1)}, bf16[512,512]{1,0:T(8,128)(2,1)}, u32[]{:S(2)}) copy-start(bf16[512,512]{1,0:T(8,128)(2,1)} %constant.91.clone.fwd_ref) | copy-start | bytes 1572868
  17.9 41.0 %copy-start.2 = (bf16[256,512]{1,0:T(8,128)(2,1)S(1)}, bf16[256,512]{1,0:T(8,128)(2,1)}, u32[]{:S(2)}) copy-start(bf16[256,512]{1,0:T(8,128)(2,1)} %constant.92.clone.inv_ref) | copy-start | bytes 786436
  29.3 29.6 %all-to-all-start = ((bf16[8,2,256,128]{3,2,1,0:T(8,128)(2,1)}), bf16[8,2,256,128]{3,2,1,0:T(8,128)(2,1)S(1)}, u32[]{:S(2)}, u32[]{:S(2)}) async-start(bf16[8,2,256,128]{3,2,1,0:T(8,128)(2,1)} %pad_maximum_fusion), calls=%async_computation | async-start | bytes 2097152 | tf_op jit(solution)/shard_map/all_to_all | solution.py:85
  32.9 104.8 %all-gather.2.cloned.1.call-start = ((), (), s32[]{:S(2)}) async-start(), calls=%async_computation.2 | async-start | bytes 4718592 | tf_op jit(solution)/shard_map/all_gather | solution.py:89
  142.3 1.3 copy-start.3
  143.7 2.7 %collective-permute-start = (bf16[2,512,512]{2,1,0:T(8,128)(2,1)S(1)}, bf16[2,512,512]{2,1,0:T(8,128)(2,1)S(1)}, u32[]{:S(2)}, u32[]{:S(2)}) collective-permute-start(bf16[2,512,512]{2,1,0:T(8,128)(2,1)S(1)} %dynamic-slice_bitcast_fusion), channel_id=1, source_target_pairs={{0,1},{1,0},{2,3},{3,2},{4,5},{5,4},{6,7},{7,6},{8,9},{9,8},{10,11... | collective-permute-start | bytes 3145736 | tf_op jit(solution)/shard_map/ppermute | solution.py:98
  148.0 14.0 %collective-permute-start.1 = (bf16[1,512,512]{2,1,0:T(8,128)(2,1)S(1)}, bf16[1,512,512]{2,1,0:T(8,128)(2,1)S(1)}, u32[]{:S(2)}, u32[]{:S(2)}) collective-permute-start(bf16[1,512,512]{2,1,0:T(8,128)(2,1)S(1)} %constant_dynamic-slice_fusion), channel_id=1, source_target_pairs={{0,2},{1,3},{2,0},{3,1},{4,6},{5,7},{6,4},{7,5},{8,10},{9,11},{10,... | collective-permute-start | bytes 1572872 | tf_op jit(solution)/shard_map/ppermute | solution.py:98
  162.2 21.6 %collective-permute-start.2 = (bf16[256,512]{1,0:T(8,128)(2,1)S(1)}, bf16[256,512]{1,0:T(8,128)(2,1)S(1)}, u32[]{:S(2)}, u32[]{:S(2)}) collective-permute-start(bf16[256,512]{1,0:T(8,128)(2,1)S(1)} %get-tuple-element.8), channel_id=1, source_target_pairs={{0,0},{1,8},{2,16},{3,24},{4,4},{5,12},{6,20},{7,28},{8,1},{9,9},{... | collective-permute-start | bytes 786440 | tf_op jit(solution)/shard_map/ppermute | solution.py:110
  165.6 23.8 %collective-permute-start.3 = (bf16[256,512]{1,0:T(8,128)(2,1)S(1)}, bf16[256,512]{1,0:T(8,128)(2,1)S(1)}, u32[]{:S(2)}, u32[]{:S(2)}) collective-permute-start(bf16[256,512]{1,0:T(8,128)(2,1)S(1)} %get-tuple-element.7), channel_id=1, source_target_pairs={{0,4},{1,12},{2,20},{3,28},{4,0},{5,8},{6,16},{7,24},{8,5},{9,13},... | collective-permute-start | bytes 786440 | tf_op jit(solution)/shard_map/ppermute | solution.py:110
Sparse Core Ops, SparseCore 0:
  63.7 74.0 all-gather.1

commit v2 on v1

v2 whole, which is shorter than its diff:
```python
import math

import jax
import jax.numpy as jnp
import numpy as np
from jax import lax
from jax.experimental import pallas as pl
from jax.experimental.pallas import tpu as pltpu
from jax.sharding import PartitionSpec as P

BF16, F32 = jnp.bfloat16, jnp.float32
MIB = 2**20


def tables(block):
    freqs = np.arange(block, dtype=np.float64)[:, None] + 0.5
    window = np.arange(-block, block, dtype=np.float64)[None, :]
    angles = math.pi / block * freqs * window
    forward = np.concatenate([np.cos(angles), -np.sin(angles)], axis=0)
    places = angles[:, block:].T
    inverse = np.concatenate([np.cos(places), -np.sin(places)], axis=1) / block
    return forward.astype(BF16), inverse.astype(BF16)


def pack_kernel(outer_ref, inner_ref, values_ref, filters_ref, out_ref):
    n, _, _, chans = out_ref.shape
    gated = (inner_ref[...].astype(F32) * values_ref[...].astype(F32)).astype(BF16)
    lags = filters_ref[...].astype(BF16)
    outer = outer_ref[...]
    for d in range(n):
        part = slice(d * chans, (d + 1) * chans)
        out_ref[d, 0] = gated[:, part]
        out_ref[d, 1] = lags[:, part]
        out_ref[d, 2] = outer[:, part]


def pack(outer_gate, inner_gate, values_in, filters, n):
    block, wide = outer_gate.shape
    tile = block // 2
    return pl.pallas_call(
        pack_kernel,
        grid=(block // tile,),
        in_specs=[pl.BlockSpec((tile, wide), lambda t: (t, 0))] * 4,
        out_specs=pl.BlockSpec((n, 3, tile, wide // n), lambda t: (0, 0, t, 0)),
        out_shape=jax.ShapeDtypeStruct((n, 3, block, wide // n), BF16),
        compiler_params=pltpu.CompilerParams(vmem_limit_bytes=32 * MIB),
        cost_estimate=pl.CostEstimate(flops=2**18, bytes_accessed=4 * MIB, transcendentals=0),
        name="pack",
    )(outer_gate, inner_gate, values_in, filters)


def conv_kernel(places, in_ref, skip_ref, fwd_ref, inv_ref, *rest):
    mixes, (xs, gs, ys) = rest[:-3], rest[-3:]
    n, _, block, chans = in_ref.shape
    for k in range(n):
        xs[k] = jnp.dot(fwd_ref[:, block:], in_ref[k, 0], preferred_element_type=F32)
        lag = jnp.dot(fwd_ref[:, block:], in_ref[k, 1], preferred_element_type=F32)
        if k:
            lag += jnp.dot(fwd_ref[:, :block], in_ref[k - 1, 1], preferred_element_type=F32)
        gs[k] = lag

    step = 8

    @pl.loop(0, block // step)
    def _(c):
        re = pl.ds(pl.multiple_of(c * step, step), step)
        im = pl.ds(pl.multiple_of(block + c * step, step), step)
        xr = [xs[k, re, :] for k in range(n)]
        xi = [xs[k, im, :] for k in range(n)]
        gr = [gs[k, re, :] for k in range(n)]
        gi = [gs[k, im, :] for k in range(n)]
        xt = [a + b for a, b in zip(xr, xi)]
        gt = [a + b for a, b in zip(gr, gi)]
        for i in range(n):
            one = xr[0] * gr[i]
            two = xi[0] * gi[i]
            three = xt[0] * gt[i]
            for k in range(1, i + 1):
                one += xr[k] * gr[i - k]
                two += xi[k] * gi[i - k]
                three += xt[k] * gt[i - k]
            ys[i, re, :] = one - two
            ys[i, im, :] = three - (one + two)

    for i in range(n):
        conv = jnp.dot(inv_ref[...], ys[i].astype(BF16), preferred_element_type=F32)
        mix = in_ref[i, 2].astype(F32) * (conv + skip_ref[...] * in_ref[i, 0].astype(F32))
        chunk, place = places[i]
        mixes[chunk][place * block : (place + 1) * block, :] = mix.astype(BF16)


def convolve(packed, skip, places):
    n, _, block, chans = packed.shape
    forward, inverse = tables(block)
    return pl.pallas_call(
        lambda *refs: conv_kernel(places, *refs),
        out_shape=[jax.ShapeDtypeStruct((n // 2 * block, chans), BF16)] * 2,
        scratch_shapes=[pltpu.VMEM((n, 2 * block, chans), F32)] * 3,
        compiler_params=pltpu.CompilerParams(vmem_limit_bytes=40 * MIB),
        cost_estimate=pl.CostEstimate(flops=2**31, bytes_accessed=4 * MIB, transcendentals=0),
        name="convolve",
    )(packed, skip, jnp.asarray(forward), jnp.asarray(inverse))


def project_kernel(rows_ref, owners_ref, *refs):
    pieces, (w_ref, keep_ref, give_ref) = refs[:-3], refs[-3:]
    total = None
    for s in range(0, len(pieces), 2):
        left = jnp.concatenate([piece[...] for piece in pieces[s : s + 2]], axis=1)
        right = jnp.concatenate([w_ref[owners_ref[t]] for t in range(s, s + 2)], axis=0)
        term = jnp.dot(left, right, preferred_element_type=F32)
        total = term if total is None else total + term
    t = pl.program_id(0)
    half = pl.num_programs(0) // 2

    @pl.when(t < half)
    def _():
        give_ref[...] = total.astype(BF16)

    @pl.when(t >= half)
    def _():
        keep_ref[...] = total.astype(BF16)


def project(pieces, owners, w_out, order, block):
    n = len(pieces)
    chans = pieces[0].shape[1]
    count = order.shape[0]
    half = count // 2
    columns = w_out.shape[1]
    part = jax.ShapeDtypeStruct((half * block, columns), BF16)
    return pl.pallas_call(
        project_kernel,
        grid_spec=pltpu.PrefetchScalarGridSpec(
            num_scalar_prefetch=2,
            grid=(count,),
            in_specs=[pl.BlockSpec((block, chans), lambda t, o, w: (o[t], 0))] * n
            + [pl.BlockSpec((n, chans, columns), lambda t, o, w: (0, 0, 0))],
            out_specs=[
                pl.BlockSpec((block, columns), lambda t, o, w: (jnp.maximum(t - half, 0), 0)),
                pl.BlockSpec((block, columns), lambda t, o, w: (jnp.minimum(t, half - 1), 0)),
            ],
        ),
        out_shape=[part, part],
        compiler_params=pltpu.CompilerParams(vmem_limit_bytes=32 * MIB),
        cost_estimate=pl.CostEstimate(
            flops=2 * count * block * n * chans * columns,
            bytes_accessed=4 * MIB,
            transcendentals=0,
        ),
        name="project",
    )(order, owners, *pieces, w_out.reshape(n, chans, columns))


def ring_of(deep, across):
    walk = []
    for a in range(across):
        column = list(range(1, deep))
        walk += [d * across + a for d in (column if a % 2 == 0 else column[::-1])]
    return walk + [a for a in reversed(range(across))]


def per_device(outer_gate, inner_gate, values_in, filters, skip_gain, w_out):
    n, m = lax.axis_size("ctx"), lax.axis_size("ch")
    j, k = lax.axis_index("ctx"), lax.axis_index("ch")
    block, wide = outer_gate.shape
    chans = wide // n
    across = n // 4
    q = n // m

    of = [[(h + 2 * deep) * across + a for deep in range(2) for a in range(across)] for h in range(2)]
    places = {r: (h, b) for h in range(2) for b, r in enumerate(of[h])}

    packed = pack(outer_gate, inner_gate, values_in, filters, n)
    packed = lax.all_to_all(packed, "ctx", 0, 0)
    skip = lax.dynamic_slice_in_dim(skip_gain, j * chans, chans, 0)[None, :]
    mixes = convolve(packed, skip, places)

    ring = ring_of(4, across)
    spot = np.argsort(np.array(ring))
    onward = [(ring[p], ring[(p + 1) % n]) for p in range(n)]
    back = [(b, a) for a, b in onward]
    me = jnp.asarray(spot.astype(np.int32))[j]
    ring_table = jnp.asarray(np.array(ring, np.int32))

    hops = [(n // 2, n // 2 - 1), (n // 2 - 1, n // 2)]
    pieces = [[mix] for mix in mixes]
    offsets = [[0], [0]]
    tips = [[mix, mix] for mix in mixes]
    for s in range(n // 2):
        for h in range(2):
            for way, route in enumerate((onward, back)):
                if s < hops[h][way]:
                    tips[h][way] = lax.ppermute(tips[h][way], "ctx", route)
                    pieces[h].append(tips[h][way])
                    offsets[h].append(-(s + 1) if way == 0 else s + 1)

    half = m // 2
    core = k % 2
    swap = [(d, d ^ 1) for d in range(m)]
    order = (jnp.arange(m, dtype=jnp.int32) + (1 - core) * half) % m
    ended = []
    for h in range(2):
        owners = ring_table[(me + jnp.array(offsets[h], jnp.int32)) % n]
        keep, give = project(pieces[h], owners, w_out, order, block)
        got = lax.ppermute(give, "ch", swap)
        kept = (keep.astype(F32) + got.astype(F32)).reshape(half, block, -1)
        bit = 1
        while bit < half:
            mine = (k // 2 // bit) % 2
            split = kept.reshape((kept.shape[0] // 2, 2) + kept.shape[1:])
            keep = lax.dynamic_index_in_dim(split, mine, 1, keepdims=False)
            give = lax.dynamic_index_in_dim(split, 1 - mine, 1, keepdims=False).astype(BF16)
            got = lax.ppermute(give, "ch", [(d, d ^ (2 * bit)) for d in range(m)])
            kept = keep + got.astype(F32)
            bit *= 2
        ended.append(kept[0].astype(BF16))

    columns = []
    for c in range(q):
        found = []
        for h in range(2):
            route = []
            for a in range(c, n, q):
                for b in range(m):
                    r = of[h][(b % 2) * half + b // 2]
                    route.append((a * m + b, r * m + a // q))
            found.append(lax.ppermute(ended[h], ("ctx", "ch"), route))
        columns.append(jnp.where((j // across) % 2 == 0, found[0], found[1]))
    return jnp.concatenate(columns, axis=1)


def solution(mesh):
    placed = (
        P("ctx", "ch"),
        P("ctx", "ch"),
        P("ctx", "ch"),
        P("ctx", "ch"),
        P("ch"),
        P("ch", "ctx"),
    )
    return jax.shard_map(
        per_device, mesh=mesh, in_specs=placed, out_specs=P("ctx", "ch"), check_vma=False
    )
```

time: 198 us -> 158 us (0.80)
  waiting for transfers between devices: 145 us -> 85.4 us
  local copies, waits for them, and re-layouts: 7.62 us -> 22 us
  starting transfers between devices: 16.9 us -> 30.9 us
  between operations: 13.6 us -> 0.27 us
  Pallas kernels: 4.66 us -> 13.7 us
  matrix products: 4.52 us -> 0 us
    all_gather x1 -> x0, waiting for transfers between devices: 74.2 us -> none  [per_device(): whole = lax.all_gather(mix, 'ctx', axis=1, tiled=True)]
    ppermute x4 -> x22, starting transfers between devices: 7.37 us -> 25 us  [the longest x14 13.6 us: per_device(): tips[h][way] = lax.ppermute(tips[h][way], 'ctx', route)]
    unnamed x16 -> x66, local copies, waits for them, and re-layouts: 4.4 us -> 20 us
    ppermute x4 -> x22, waiting for transfers between devices: 36.5 us -> 48.5 us  [the longest x14 25.8 us: per_device(): tips[h][way] = lax.ppermute(tips[h][way], 'ctx', route)]
    pallas_call x1 -> x4, Pallas kernels: 4.66 us -> 13.7 us  [the longest x2 8.44 us: project(): pl.pallas_call(project_kernel, grid_spec=pltpu.PrefetchScalarGridSpec(num...]
    dot_general x1 -> x0, matrix products: 4.52 us -> none  [per_device(): jnp.dot(whole, w_out, preferred_element_type=jnp.float32)]
    all_to_all x2 -> x1, starting transfers between devices: 9.47 us -> 5.97 us  [per_device(): packed = lax.all_to_all(packed, 'ctx', 0, 0)]
    all_to_all x2 -> x1, waiting for transfers between devices: 34.3 us -> 36.9 us  [per_device(): packed = lax.all_to_all(packed, 'ctx', 0, 0)]
  transfers between devices with their start and end apart: 7 -> 23, of which waited for: 7 -> 14; matrix products, arithmetic and copies ran while one was open for 3% -> 3% of each run, Pallas kernels for 0% -> 5%
where the time goes in v2:
time: 158 us; the launch traced here: 156 us
  waiting for transfers between devices  85.4 us (54%)
  starting transfers between devices  30.9 us (20%)
  local copies, waits for them, and re-layouts  22 us (14%)
  Pallas kernels  13.7 us (9%)
  other arithmetic  4.15 us (3%)
    all_to_all x1, waiting for transfers between devices, per_device(): packed = lax.all_to_all(packed, 'ctx', 0, 0)  36.9 us
    ppermute x14, waiting for transfers between devices, per_device(): tips[h][way] = lax.ppermute(tips[h][way], 'ctx', route)  25.8 us
    unnamed x66, local copies, waits for them, and re-layouts  20 us
    ppermute x4, waiting for transfers between devices, per_device(): found.append(lax.ppermute(ended[h], ('ctx', 'ch'), route))  16.7 us
    ppermute x14, starting transfers between devices, per_device(): tips[h][way] = lax.ppermute(tips[h][way], 'ctx', route)  13.6 us
    ppermute x4, starting transfers between devices, per_device(): found.append(lax.ppermute(ended[h], ('ctx', 'ch'), route))  9.42 us
    pallas_call x2, Pallas kernels, project(): pl.pallas_call(project_kernel, grid_spec=pltpu.PrefetchScalarGridSpec(num...  8.44 us
    all_to_all x1, starting transfers between devices, per_device(): packed = lax.all_to_all(packed, 'ctx', 0, 0)  5.97 us
  transfers between devices with their start and end apart: 23, of which 14 were waited for; matrix products, arithmetic and copies ran while one was open for 3% of the time, Pallas kernels for 5%

profile of v2, /device:TPU:2, one launch (start us, length us, event | category | flops | bytes accessed | tf_op | source)
XLA Modules:
  0.0 156.4 jit_solution(3129375805377327483)
XLA Ops:
  4.4 1.4 pack.1
  5.7 6.0 %all-to-all-start = ((bf16[8,3,256,128]{3,2,1,0:T(8,128)(2,1)}), bf16[8,3,256,128]{3,2,1,0:T(8,128)(2,1)S(1)}, u32[]{:S(2)}, u32[]{:S(2)}) async-start(bf16[8,3,256,128]{3,2,1,0:T(8,128)(2,1)} %pack.1), calls=%async_computation | async-start | bytes 3145728 | tf_op jit(solution)/shard_map/all_to_all | solution.py:175
  11.8 36.9 %all-to-all-done.refs_0_ = bf16[8,3,256,128]{3,2,1,0:T(8,128)(2,1)S(1)} async-done(((bf16[8,3,256,128]{3,2,1,0:T(8,128)(2,1)}), bf16[8,3,256,128]{3,2,1,0:T(8,128)(2,1)S(1)}, u32[]{:S(2)}, u32[]{:S(2)}) %all-to-all-start) | async-done | bytes 1572896 | tf_op jit(solution)/shard_map/all_to_all | solution.py:175
  49.7 3.9 %convolve.1 = (bf16[1024,128]{1,0:T(8,128)(2,1)S(1)}, bf16[1024,128]{1,0:T(8,128)(2,1)S(1)}) custom-call(bf16[8,3,256,128]{3,2,1,0:T(8,128)(2,1)S(1)} %all-to-all-done.refs_0_, f32[1,128]{1,0:T(1,128)S(1)} %dynamic-slice_bitcast_fusion.refs_1_, bf16[512,512]{1,0:T(8,128)(2,1)S(1)} %copy-done.26, bf16[256,512]{1,0:T(8,128)(2,1)S(1)} %copy-done.27), custom_call_target="tpu_custom_call" | custom-call | flops 2147483648 | bytes 4194304 | tf_op jit(solution)/shard_map/convolve/pallas_call | solution.py:95
  53.6 1.5 collective-permute-start.11
  55.7 4.9 %collective-permute-done.11.refs_2_ = bf16[1024,128]{1,0:T(8,128)(2,1)S(1)} collective-permute-done((bf16[1024,128]{1,0:T(8,128)(2,1)S(1)}, bf16[1024,128]{1,0:T(8,128)(2,1)S(1)}, u32[]{:S(2)}, u32[]{:S(2)}) %collective-permute-start.11) | collective-permute-done | bytes 262176 | tf_op jit(solution)/shard_map/ppermute | solution.py:194
  60.6 1.8 %collective-permute-start.13 = (bf16[1024,128]{1,0:T(8,128)(2,1)S(1)}, bf16[1024,128]{1,0:T(8,128)(2,1)S(1)}, u32[]{:S(2)}, u32[]{:S(2)}) collective-permute-start(bf16[1024,128]{1,0:T(8,128)(2,1)S(1)} %collective-permute-done.11.refs_2_), channel_id=1, source_target_pairs={{16,8},{24,16},{28,24},{20,28},{12,20},{4,12},{0,4},{8,0},{17,9},{... | collective-permute-start | bytes 786440 | tf_op jit(solution)/shard_map/ppermute | solution.py:194
  64.0 2.9 %collective-permute-done.13.refs_4_ = bf16[1024,128]{1,0:T(8,128)(2,1)S(1)} collective-permute-done((bf16[1024,128]{1,0:T(8,128)(2,1)S(1)}, bf16[1024,128]{1,0:T(8,128)(2,1)S(1)}, u32[]{:S(2)}, u32[]{:S(2)}) %collective-permute-start.13) | collective-permute-done | bytes 262176 | tf_op jit(solution)/shard_map/ppermute | solution.py:194
  67.0 2.1 %collective-permute-start.15 = (bf16[1024,128]{1,0:T(8,128)(2,1)S(1)}, bf16[1024,128]{1,0:T(8,128)(2,1)}, u32[]{:S(2)}, u32[]{:S(2)}) collective-permute-start(bf16[1024,128]{1,0:T(8,128)(2,1)S(1)} %collective-permute-done.13.refs_4_), channel_id=1, source_target_pairs={{16,8},{24,16},{28,24},{20,28},{12,20},{4,12},{0,4},{8,0},{17,9},{... | collective-permute-start | bytes 786440 | tf_op jit(solution)/shard_map/ppermute | solution.py:194
  70.0 1.6 %collective-permute-done.refs_1_ = bf16[1024,128]{1,0:T(8,128)(2,1)S(1)} collective-permute-done((bf16[1024,128]{1,0:T(8,128)(2,1)S(1)}, bf16[1024,128]{1,0:T(8,128)(2,1)S(1)}, u32[]{:S(2)}, u32[]{:S(2)}) %collective-permute-start) | collective-permute-done | bytes 262176 | tf_op jit(solution)/shard_map/ppermute | solution.py:194
  72.4 4.9 %collective-permute-done.12.refs_3_ = bf16[1024,128]{1,0:T(8,128)(2,1)} collective-permute-done((bf16[1024,128]{1,0:T(8,128)(2,1)S(1)}, bf16[1024,128]{1,0:T(8,128)(2,1)}, u32[]{:S(2)}, u32[]{:S(2)}) %collective-permute-start.12) | collective-permute-done | bytes 262176 | tf_op jit(solution)/shard_map/ppermute | solution.py:194
  77.3 2.0 %collective-permute-start.16 = (bf16[1024,128]{1,0:T(8,128)(2,1)}, bf16[1024,128]{1,0:T(8,128)(2,1)S(1)}, u32[]{:S(2)}, u32[]{:S(2)}) collective-permute-start(bf16[1024,128]{1,0:T(8,128)(2,1)} %collective-permute-done.15.refs_6_), channel_id=1, source_target_pairs={{16,8},{24,16},{28,24},{20,28},{12,20},{4,12},{0,4},{8,0},{17,9},{... | collective-permute-start | bytes 786440 | tf_op jit(solution)/shard_map/ppermute | solution.py:194
  80.0 2.1 %collective-permute-done.1.refs_2_ = bf16[1024,128]{1,0:T(8,128)(2,1)S(1)} collective-permute-done((bf16[1024,128]{1,0:T(8,128)(2,1)S(1)}, bf16[1024,128]{1,0:T(8,128)(2,1)S(1)}, u32[]{:S(2)}, u32[]{:S(2)}) %collective-permute-start.1) | collective-permute-done | bytes 262176 | tf_op jit(solution)/shard_map/ppermute | solution.py:194
  82.1 1.7 %collective-permute-start.3 = (bf16[1024,128]{1,0:T(8,128)(2,1)S(1)}, bf16[1024,128]{1,0:T(8,128)(2,1)}, u32[]{:S(2)}, u32[]{:S(2)}) collective-permute-start(bf16[1024,128]{1,0:T(8,128)(2,1)S(1)} %collective-permute-done.1.refs_2_), channel_id=1, source_target_pairs={{16,8},{24,16},{28,24},{20,28},{12,20},{4,12},{0,4},{8,0},{17,9},{... | collective-permute-start | bytes 786440 | tf_op jit(solution)/shard_map/ppermute | solution.py:194
  84.9 3.2 %collective-permute-done.14.refs_5_ = bf16[1024,128]{1,0:T(8,128)(2,1)S(1)} collective-permute-done((bf16[1024,128]{1,0:T(8,128)(2,1)}, bf16[1024,128]{1,0:T(8,128)(2,1)S(1)}, u32[]{:S(2)}, u32[]{:S(2)}) %collective-permute-start.14) | collective-permute-done | bytes 262176 | tf_op jit(solution)/shard_map/ppermute | solution.py:194
  95.2 3.8 %project.3 = (bf16[512,512]{1,0:T(8,128)(2,1)S(1)}, bf16[512,512]{1,0:T(8,128)(2,1)S(1)}) custom-call(s32[4]{0:T(128)S(1)} %and_select_fusion.2.rows_ref, s32[8]{0:T(128)S(1)} %gather_fusion.1, bf16[1024,128]{1,0:T(8,128)(2,1)S(1)} %copy-done.9, bf16[1024,128]{1,0:T(8,128)(2,1)S(1)} %copy-done.15, bf16[1024,128]{1,0:T(8,128)(2,1)S(1)} %copy-done.13, ...), custom_call_target="tpu_custom_call" | custom-call | flops 1073741824 | bytes 4194304 | tf_op jit(solution)/shard_map/project/pallas_call | solution.py:132
  99.2 2.0 %collective-permute-start.6 = (bf16[1024,128]{1,0:T(8,128)(2,1)}, bf16[1024,128]{1,0:T(8,128)(2,1)S(1)}, u32[]{:S(2)}, u32[]{:S(2)}) collective-permute-start(bf16[1024,128]{1,0:T(8,128)(2,1)} %collective-permute-done.4.refs_5_), channel_id=1, source_target_pairs={{8,16},{16,24},{24,28},{28,20},{20,12},{12,4},{4,0},{0,8},{9,17},{... | collective-permute-start | bytes 786440 | tf_op jit(solution)/shard_map/ppermute | solution.py:194
  101.9 6.2 %collective-permute-done.5.refs_6_ = bf16[1024,128]{1,0:T(8,128)(2,1)S(1)} collective-permute-done((bf16[1024,128]{1,0:T(8,128)(2,1)}, bf16[1024,128]{1,0:T(8,128)(2,1)S(1)}, u32[]{:S(2)}, u32[]{:S(2)}) %collective-permute-start.5) | collective-permute-done | bytes 262176 | tf_op jit(solution)/shard_map/ppermute | solution.py:194
  113.2 4.6 %project.2 = (bf16[512,512]{1,0:T(8,128)(2,1)S(1)}, bf16[512,512]{1,0:T(8,128)(2,1)}) custom-call(s32[4]{0:T(128)S(1)} %and_select_fusion.2.rows_ref, s32[8]{0:T(128)S(1)} %gather_fusion, bf16[1024,128]{1,0:T(8,128)(2,1)S(1)} %get-tuple-element.11.refs_0_, bf16[1024,128]{1,0:T(8,128)(2,1)S(1)} %collective-permute-done.refs_1_, ...), custom_call_target="tpu_custom_call" | custom-call | flops 1073741824 | bytes 4194304 | tf_op jit(solution)/shard_map/project/pallas_call | solution.py:132
  123.4 5.0 %collective-permute-done.18 = bf16[1,256,512]{2,1,0:T(8,128)(2,1)S(1)} collective-permute-done((bf16[1,256,512]{2,1,0:T(8,128)(2,1)S(1)}, bf16[1,256,512]{2,1,0:T(8,128)(2,1)S(1)}, u32[]{:S(2)}, u32[]{:S(2)}) %collective-permute-start.18) | collective-permute-done | bytes 262176 | tf_op jit(solution)/shard_map/ppermute | solution.py:214
  128.4 4.3 %collective-permute-start.19 = (bf16[256,512]{1,0:T(8,128)(2,1)S(1)}, bf16[256,512]{1,0:T(8,128)(2,1)S(1)}, u32[]{:S(2)}, u32[]{:S(2)}) collective-permute-start(bf16[256,512]{1,0:T(8,128)(2,1)S(1)} %fusion.5), channel_id=1, source_target_pairs={{0,8},{1,24},{2,12},{3,28},{8,9},{9,25},{10,13},{11,29},{16,10},{1... | collective-permute-start | bytes 786440 | tf_op jit(solution)/shard_map/ppermute | solution.py:228
  133.6 3.1 %collective-permute-start.9 = (bf16[256,512]{1,0:T(8,128)(2,1)S(1)}, bf16[256,512]{1,0:T(8,128)(2,1)S(1)}, u32[]{:S(2)}, u32[]{:S(2)}) collective-permute-start(bf16[256,512]{1,0:T(8,128)(2,1)S(1)} %fusion.4), channel_id=1, source_target_pairs={{0,0},{1,16},{2,4},{3,20},{8,1},{9,17},{10,5},{11,21},{16,2},{17,1... | collective-permute-start | bytes 786440 | tf_op jit(solution)/shard_map/ppermute | solution.py:228
  139.0 7.6 %collective-permute-done.9 = bf16[256,512]{1,0:T(8,128)(2,1)S(1)} collective-permute-done((bf16[256,512]{1,0:T(8,128)(2,1)S(1)}, bf16[256,512]{1,0:T(8,128)(2,1)S(1)}, u32[]{:S(2)}, u32[]{:S(2)}) %collective-permute-start.9) | collective-permute-done | bytes 262176 | tf_op jit(solution)/shard_map/ppermute | solution.py:228
  146.7 8.8 %collective-permute-done.20 = bf16[256,512]{1,0:T(8,128)(2,1)S(1)} collective-permute-done((bf16[256,512]{1,0:T(8,128)(2,1)S(1)}, bf16[256,512]{1,0:T(8,128)(2,1)S(1)}, u32[]{:S(2)}, u32[]{:S(2)}) %collective-permute-start.20) | collective-permute-done | bytes 262176 | tf_op jit(solution)/shard_map/ppermute | solution.py:228
  (109 shorter events, 33.8 us)
Async XLA Ops:
  5.7 43.0 %all-to-all-start = ((bf16[8,3,256,128]{3,2,1,0:T(8,128)(2,1)}), bf16[8,3,256,128]{3,2,1,0:T(8,128)(2,1)S(1)}, u32[]{:S(2)}, u32[]{:S(2)}) async-start(bf16[8,3,256,128]{3,2,1,0:T(8,128)(2,1)} %pack.1), calls=%async_computation | async-start | bytes 3145728 | tf_op jit(solution)/shard_map/all_to_all | solution.py:175
  11.8 77.8 %copy-start.5 = (bf16[1024,512]{1,0:T(8,128)(2,1)S(1)}, bf16[1024,512]{1,0:T(8,128)(2,1)}, u32[]{:S(2)}) copy-start(bf16[1024,512]{1,0:T(8,128)(2,1)} %param.17) | copy-start | bytes 3145732
  53.6 7.0 %collective-permute-start.11 = (bf16[1024,128]{1,0:T(8,128)(2,1)S(1)}, bf16[1024,128]{1,0:T(8,128)(2,1)S(1)}, u32[]{:S(2)}, u32[]{:S(2)}) collective-permute-start(bf16[1024,128]{1,0:T(8,128)(2,1)S(1)} %get-tuple-element.14.refs_0_), channel_id=1, source_target_pairs={{16,8},{24,16},{28,24},{20,28},{12,20},{4,12},{0,4},{8,0},{17,9},{... | collective-permute-start | bytes 786440 | tf_op jit(solution)/shard_map/ppermute | solution.py:194
  55.1 7.5 %collective-permute-start.10 = (bf16[1024,128]{1,0:T(8,128)(2,1)S(1)}, bf16[1024,128]{1,0:T(8,128)(2,1)S(1)}, u32[]{:S(2)}, u32[]{:S(2)}) collective-permute-start(bf16[1024,128]{1,0:T(8,128)(2,1)S(1)} %get-tuple-element.14.refs_0_), channel_id=1, source_target_pairs={{8,16},{16,24},{24,28},{28,20},{20,12},{12,4},{4,0},{0,8},{9,17},{... | collective-permute-start | bytes 786440 | tf_op jit(solution)/shard_map/ppermute | solution.py:194
  60.6 6.4 %collective-permute-start.13 = (bf16[1024,128]{1,0:T(8,128)(2,1)S(1)}, bf16[1024,128]{1,0:T(8,128)(2,1)S(1)}, u32[]{:S(2)}, u32[]{:S(2)}) collective-permute-start(bf16[1024,128]{1,0:T(8,128)(2,1)S(1)} %collective-permute-done.11.refs_2_), channel_id=1, source_target_pairs={{16,8},{24,16},{28,24},{20,28},{12,20},{4,12},{0,4},{8,0},{17,9},{... | collective-permute-start | bytes 786440 | tf_op jit(solution)/shard_map/ppermute | solution.py:194
  62.4 9.2 %collective-permute-start = (bf16[1024,128]{1,0:T(8,128)(2,1)S(1)}, bf16[1024,128]{1,0:T(8,128)(2,1)S(1)}, u32[]{:S(2)}, u32[]{:S(2)}) collective-permute-start(bf16[1024,128]{1,0:T(8,128)(2,1)S(1)} %get-tuple-element.11.refs_0_), channel_id=1, source_target_pairs={{8,16},{16,24},{24,28},{28,20},{20,12},{12,4},{4,0},{0,8},{9,17},{... | collective-permute-start | bytes 786440 | tf_op jit(solution)/shard_map/ppermute | solution.py:194
  62.6 14.7 %collective-permute-start.12 = (bf16[1024,128]{1,0:T(8,128)(2,1)S(1)}, bf16[1024,128]{1,0:T(8,128)(2,1)}, u32[]{:S(2)}, u32[]{:S(2)}) collective-permute-start(bf16[1024,128]{1,0:T(8,128)(2,1)S(1)} %collective-permute-done.10.refs_1_), channel_id=1, source_target_pairs={{8,16},{16,24},{24,28},{28,20},{20,12},{12,4},{4,0},{0,8},{9,17},{... | collective-permute-start | bytes 786440 | tf_op jit(solution)/shard_map/ppermute | solution.py:194
  67.0 10.4 %collective-permute-start.15 = (bf16[1024,128]{1,0:T(8,128)(2,1)S(1)}, bf16[1024,128]{1,0:T(8,128)(2,1)}, u32[]{:S(2)}, u32[]{:S(2)}) collective-permute-start(bf16[1024,128]{1,0:T(8,128)(2,1)S(1)} %collective-permute-done.13.refs_4_), channel_id=1, source_target_pairs={{16,8},{24,16},{28,24},{20,28},{12,20},{4,12},{0,4},{8,0},{17,9},{... | collective-permute-start | bytes 786440 | tf_op jit(solution)/shard_map/ppermute | solution.py:194
  69.8 12.3 %collective-permute-start.1 = (bf16[1024,128]{1,0:T(8,128)(2,1)S(1)}, bf16[1024,128]{1,0:T(8,128)(2,1)S(1)}, u32[]{:S(2)}, u32[]{:S(2)}) collective-permute-start(bf16[1024,128]{1,0:T(8,128)(2,1)S(1)} %get-tuple-element.11.refs_0_), channel_id=1, source_target_pairs={{16,8},{24,16},{28,24},{20,28},{12,20},{4,12},{0,4},{8,0},{17,9},{... | collective-permute-start | bytes 786440 | tf_op jit(solution)/shard_map/ppermute | solution.py:194
  71.6 12.2 %collective-permute-start.2 = (bf16[1024,128]{1,0:T(8,128)(2,1)S(1)}, bf16[1024,128]{1,0:T(8,128)(2,1)S(1)}, u32[]{:S(2)}, u32[]{:S(2)}) collective-permute-start(bf16[1024,128]{1,0:T(8,128)(2,1)S(1)} %collective-permute-done.refs_1_), channel_id=1, source_target_pairs={{8,16},{16,24},{24,28},{28,20},{20,12},{12,4},{4,0},{0,8},{9,17},{... | collective-permute-start | bytes 786440 | tf_op jit(solution)/shard_map/ppermute | solution.py:194
  77.3 10.8 %collective-permute-start.14 = (bf16[1024,128]{1,0:T(8,128)(2,1)}, bf16[1024,128]{1,0:T(8,128)(2,1)S(1)}, u32[]{:S(2)}, u32[]{:S(2)}) collective-permute-start(bf16[1024,128]{1,0:T(8,128)(2,1)} %collective-permute-done.12.refs_3_), channel_id=1, source_target_pairs={{8,16},{16,24},{24,28},{28,20},{20,12},{12,4},{4,0},{0,8},{9,17},{... | collective-permute-start | bytes 786440 | tf_op jit(solution)/shard_map/ppermute | solution.py:194
  77.3 11.5 %collective-permute-start.16 = (bf16[1024,128]{1,0:T(8,128)(2,1)}, bf16[1024,128]{1,0:T(8,128)(2,1)S(1)}, u32[]{:S(2)}, u32[]{:S(2)}) collective-permute-start(bf16[1024,128]{1,0:T(8,128)(2,1)} %collective-permute-done.15.refs_6_), channel_id=1, source_target_pairs={{16,8},{24,16},{28,24},{20,28},{12,20},{4,12},{0,4},{8,0},{17,9},{... | collective-permute-start | bytes 786440 | tf_op jit(solution)/shard_map/ppermute | solution.py:194
  82.1 17.0 %collective-permute-start.3 = (bf16[1024,128]{1,0:T(8,128)(2,1)S(1)}, bf16[1024,128]{1,0:T(8,128)(2,1)}, u32[]{:S(2)}, u32[]{:S(2)}) collective-permute-start(bf16[1024,128]{1,0:T(8,128)(2,1)S(1)} %collective-permute-done.1.refs_2_), channel_id=1, source_target_pairs={{16,8},{24,16},{28,24},{20,28},{12,20},{4,12},{0,4},{8,0},{17,9},{... | collective-permute-start | bytes 786440 | tf_op jit(solution)/shard_map/ppermute | solution.py:194
  83.8 15.4 %collective-permute-start.4 = (bf16[1024,128]{1,0:T(8,128)(2,1)S(1)}, bf16[1024,128]{1,0:T(8,128)(2,1)}, u32[]{:S(2)}, u32[]{:S(2)}) collective-permute-start(bf16[1024,128]{1,0:T(8,128)(2,1)S(1)} %collective-permute-done.2.refs_3_), channel_id=1, source_target_pairs={{8,16},{16,24},{24,28},{28,20},{20,12},{12,4},{4,0},{0,8},{9,17},{... | collective-permute-start | bytes 786440 | tf_op jit(solution)/shard_map/ppermute | solution.py:194
  99.1 18.8 %collective-permute-start.17 = (bf16[512,512]{1,0:T(8,128)(2,1)S(1)}, bf16[512,512]{1,0:T(8,128)(2,1)}, u32[]{:S(2)}, u32[]{:S(2)}) collective-permute-start(bf16[512,512]{1,0:T(8,128)(2,1)S(1)} %get-tuple-element.16), channel_id=1, source_target_pairs={{0,1},{1,0},{2,3},{3,2},{4,5},{5,4},{6,7},{7,6},{8,9},{9,8},{10,11... | collective-permute-start | bytes 1572872 | tf_op jit(solution)/shard_map/ppermute | solution.py:206
  99.1 8.9 %collective-permute-start.5 = (bf16[1024,128]{1,0:T(8,128)(2,1)}, bf16[1024,128]{1,0:T(8,128)(2,1)S(1)}, u32[]{:S(2)}, u32[]{:S(2)}) collective-permute-start(bf16[1024,128]{1,0:T(8,128)(2,1)} %collective-permute-done.3.refs_4_), channel_id=1, source_target_pairs={{16,8},{24,16},{28,24},{20,28},{12,20},{4,12},{0,4},{8,0},{17,9},{... | collective-permute-start | bytes 786440 | tf_op jit(solution)/shard_map/ppermute | solution.py:194
  99.2 9.5 %collective-permute-start.6 = (bf16[1024,128]{1,0:T(8,128)(2,1)}, bf16[1024,128]{1,0:T(8,128)(2,1)S(1)}, u32[]{:S(2)}, u32[]{:S(2)}) collective-permute-start(bf16[1024,128]{1,0:T(8,128)(2,1)} %collective-permute-done.4.refs_5_), channel_id=1, source_target_pairs={{8,16},{16,24},{24,28},{28,20},{20,12},{12,4},{4,0},{0,8},{9,17},{... | collective-permute-start | bytes 786440 | tf_op jit(solution)/shard_map/ppermute | solution.py:194
  117.9 2.1 %collective-permute-start.7 = (bf16[512,512]{1,0:T(8,128)(2,1)}, bf16[512,512]{1,0:T(8,128)(2,1)S(1)}, u32[]{:S(2)}, u32[]{:S(2)}) collective-permute-start(bf16[512,512]{1,0:T(8,128)(2,1)} %get-tuple-element.13), channel_id=1, source_target_pairs={{0,1},{1,0},{2,3},{3,2},{4,5},{5,4},{6,7},{7,6},{8,9},{9,8},{10,11... | collective-permute-start | bytes 1572872 | tf_op jit(solution)/shard_map/ppermute | solution.py:206
  119.2 9.2 %collective-permute-start.18 = (bf16[1,256,512]{2,1,0:T(8,128)(2,1)S(1)}, bf16[1,256,512]{2,1,0:T(8,128)(2,1)S(1)}, u32[]{:S(2)}, u32[]{:S(2)}) collective-permute-start(bf16[1,256,512]{2,1,0:T(8,128)(2,1)S(1)} %fusion.3), channel_id=1, source_target_pairs={{0,2},{1,3},{2,0},{3,1},{4,6},{5,7},{6,4},{7,5},{8,10},{9,11},{10,... | collective-permute-start | bytes 786440 | tf_op jit(solution)/shard_map/ppermute | solution.py:214
  122.1 11.5 %collective-permute-start.8 = (bf16[1,256,512]{2,1,0:T(8,128)(2,1)S(1)}, bf16[1,256,512]{2,1,0:T(8,128)(2,1)S(1)}, u32[]{:S(2)}, u32[]{:S(2)}) collective-permute-start(bf16[1,256,512]{2,1,0:T(8,128)(2,1)S(1)} %fusion.2), channel_id=1, source_target_pairs={{0,2},{1,3},{2,0},{3,1},{4,6},{5,7},{6,4},{7,5},{8,10},{9,11},{10,... | collective-permute-start | bytes 786440 | tf_op jit(solution)/shard_map/ppermute | solution.py:214
  128.4 10.6 %collective-permute-start.19 = (bf16[256,512]{1,0:T(8,128)(2,1)S(1)}, bf16[256,512]{1,0:T(8,128)(2,1)S(1)}, u32[]{:S(2)}, u32[]{:S(2)}) collective-permute-start(bf16[256,512]{1,0:T(8,128)(2,1)S(1)} %fusion.5), channel_id=1, source_target_pairs={{0,8},{1,24},{2,12},{3,28},{8,9},{9,25},{10,13},{11,29},{16,10},{1... | collective-permute-start | bytes 786440 | tf_op jit(solution)/shard_map/ppermute | solution.py:228
  133.6 13.0 %collective-permute-start.9 = (bf16[256,512]{1,0:T(8,128)(2,1)S(1)}, bf16[256,512]{1,0:T(8,128)(2,1)S(1)}, u32[]{:S(2)}, u32[]{:S(2)}) collective-permute-start(bf16[256,512]{1,0:T(8,128)(2,1)S(1)} %fusion.4), channel_id=1, source_target_pairs={{0,0},{1,16},{2,4},{3,20},{8,1},{9,17},{10,5},{11,21},{16,2},{17,1... | collective-permute-start | bytes 786440 | tf_op jit(solution)/shard_map/ppermute | solution.py:228
  136.8 9.9 %collective-permute-start.21 = (bf16[256,512]{1,0:T(8,128)(2,1)S(1)}, bf16[256,512]{1,0:T(8,128)(2,1)S(1)}, u32[]{:S(2)}, u32[]{:S(2)}) collective-permute-start(bf16[256,512]{1,0:T(8,128)(2,1)S(1)} %fusion.5), channel_id=1, source_target_pairs={{4,8},{5,24},{6,12},{7,28},{12,9},{13,25},{14,13},{15,29},{20,10},... | collective-permute-start | bytes 786440 | tf_op jit(solution)/shard_map/ppermute | solution.py:228
  137.5 18.0 %collective-permute-start.20 = (bf16[256,512]{1,0:T(8,128)(2,1)S(1)}, bf16[256,512]{1,0:T(8,128)(2,1)S(1)}, u32[]{:S(2)}, u32[]{:S(2)}) collective-permute-start(bf16[256,512]{1,0:T(8,128)(2,1)S(1)} %fusion.4), channel_id=1, source_target_pairs={{4,0},{5,16},{6,4},{7,20},{12,1},{13,17},{14,5},{15,21},{20,2},{21... | collective-permute-start | bytes 786440 | tf_op jit(solution)/shard_map/ppermute | solution.py:228
  (32 other events, 286.0 us)

commit v3 on v2

--- a/solution.py
+++ b/solution.py
@@ -43,7 +43,7 @@
         in_specs=[pl.BlockSpec((tile, wide), lambda t: (t, 0))] * 4,
         out_specs=pl.BlockSpec((n, 3, tile, wide // n), lambda t: (0, 0, t, 0)),
         out_shape=jax.ShapeDtypeStruct((n, 3, block, wide // n), BF16),
-        compiler_params=pltpu.CompilerParams(vmem_limit_bytes=32 * MIB),
+        compiler_params=pltpu.CompilerParams(vmem_limit_bytes=60 * MIB),
         cost_estimate=pl.CostEstimate(flops=2**18, bytes_accessed=4 * MIB, transcendentals=0),
         name="pack",
     )(outer_gate, inner_gate, values_in, filters)
@@ -96,18 +96,19 @@
         lambda *refs: conv_kernel(places, *refs),
         out_shape=[jax.ShapeDtypeStruct((n // 2 * block, chans), BF16)] * 2,
         scratch_shapes=[pltpu.VMEM((n, 2 * block, chans), F32)] * 3,
-        compiler_params=pltpu.CompilerParams(vmem_limit_bytes=40 * MIB),
+        compiler_params=pltpu.CompilerParams(vmem_limit_bytes=16 * MIB),
         cost_estimate=pl.CostEstimate(flops=2**31, bytes_accessed=4 * MIB, transcendentals=0),
         name="convolve",
     )(packed, skip, jnp.asarray(forward), jnp.asarray(inverse))
 
 
-def project_kernel(rows_ref, owners_ref, *refs):
+def project_kernel(here_ref, table_ref, *refs):
     pieces, (w_ref, keep_ref, give_ref) = refs[:-3], refs[-3:]
+    n = len(pieces)
     total = None
     for s in range(0, len(pieces), 2):
         left = jnp.concatenate([piece[...] for piece in pieces[s : s + 2]], axis=1)
-        right = jnp.concatenate([w_ref[owners_ref[t]] for t in range(s, s + 2)], axis=0)
+        right = jnp.concatenate([w_ref[table_ref[here_ref[0] * n + t]] for t in range(s, s + 2)], axis=0)
         term = jnp.dot(left, right, preferred_element_type=F32)
         total = term if total is None else total + term
     t = pl.program_id(0)
@@ -122,11 +123,15 @@
         keep_ref[...] = total.astype(BF16)
 
 
-def project(pieces, owners, w_out, order, block):
+def project(pieces, here, table, w_out, block):
     n = len(pieces)
+    count = pieces[0].shape[0] // block
     chans = pieces[0].shape[1]
-    count = order.shape[0]
     half = count // 2
+
+    def rows(t, here, table):
+        return (lax.rem(t + (1 - lax.rem(here[1], 2)) * half, count), 0)
+
     columns = w_out.shape[1]
     part = jax.ShapeDtypeStruct((half * block, columns), BF16)
     return pl.pallas_call(
@@ -134,7 +139,7 @@
         grid_spec=pltpu.PrefetchScalarGridSpec(
             num_scalar_prefetch=2,
             grid=(count,),
-            in_specs=[pl.BlockSpec((block, chans), lambda t, o, w: (o[t], 0))] * n
+            in_specs=[pl.BlockSpec((block, chans), rows)] * n
             + [pl.BlockSpec((n, chans, columns), lambda t, o, w: (0, 0, 0))],
             out_specs=[
                 pl.BlockSpec((block, columns), lambda t, o, w: (jnp.maximum(t - half, 0), 0)),
@@ -142,14 +147,14 @@
             ],
         ),
         out_shape=[part, part],
-        compiler_params=pltpu.CompilerParams(vmem_limit_bytes=32 * MIB),
+        compiler_params=pltpu.CompilerParams(vmem_limit_bytes=10 * MIB),
         cost_estimate=pl.CostEstimate(
             flops=2 * count * block * n * chans * columns,
             bytes_accessed=4 * MIB,
             transcendentals=0,
         ),
         name="project",
-    )(order, owners, *pieces, w_out.reshape(n, chans, columns))
+    )(here, table, *pieces, w_out.reshape(n, chans, columns))
 
 
 def ring_of(deep, across):
@@ -180,8 +185,7 @@
     spot = np.argsort(np.array(ring))
     onward = [(ring[p], ring[(p + 1) % n]) for p in range(n)]
     back = [(b, a) for a, b in onward]
-    me = jnp.asarray(spot.astype(np.int32))[j]
-    ring_table = jnp.asarray(np.array(ring, np.int32))
+    here = jnp.stack([j, k]).astype(jnp.int32)
 
     hops = [(n // 2, n // 2 - 1), (n // 2 - 1, n // 2)]
     pieces = [[mix] for mix in mixes]
@@ -196,13 +200,11 @@
                     offsets[h].append(-(s + 1) if way == 0 else s + 1)
 
     half = m // 2
-    core = k % 2
     swap = [(d, d ^ 1) for d in range(m)]
-    order = (jnp.arange(m, dtype=jnp.int32) + (1 - core) * half) % m
     ended = []
     for h in range(2):
-        owners = ring_table[(me + jnp.array(offsets[h], jnp.int32)) % n]
-        keep, give = project(pieces[h], owners, w_out, order, block)
+        owners = np.array([[ring[(spot[a] + o) % n] for o in offsets[h]] for a in range(n)], np.int32)
+        keep, give = project(pieces[h], here, jnp.asarray(owners.reshape(-1)), w_out, block)
         got = lax.ppermute(give, "ch", swap)
         kept = (keep.astype(F32) + got.astype(F32)).reshape(half, block, -1)
         bit = 1

time: 158 us -> 150 us (0.949)
  local copies, waits for them, and re-layouts: 22 us -> 13.1 us
    unnamed x66 -> x42, local copies, waits for them, and re-layouts: 20 us -> 12.9 us
    pallas_call x2, Pallas kernels: 8.44 us -> 6.38 us  [project(): pl.pallas_call(project_kernel, grid_spec=pltpu.PrefetchScalarGridSpec(num...]
  transfers between devices with their start and end apart: 23 -> 23, of which waited for: 14 -> 15; matrix products, arithmetic and copies ran while one was open for 3% -> 2% of each run, Pallas kernels for 5% -> 4%
where the time goes in v3:
time: 150 us; the launch traced here: 149 us
  waiting for transfers between devices  86.6 us (58%)
  starting transfers between devices  32.3 us (22%)
  local copies, waits for them, and re-layouts  13.1 us (9%)
  Pallas kernels  13 us (9%)
  other arithmetic  3.52 us (2%)
    all_to_all x1, waiting for transfers between devices, per_device(): packed = lax.all_to_all(packed, 'ctx', 0, 0)  36.9 us
    ppermute x14, waiting for transfers between devices, per_device(): tips[h][way] = lax.ppermute(tips[h][way], 'ctx', route)  27 us
    ppermute x4, waiting for transfers between devices, per_device(): found.append(lax.ppermute(ended[h], ('ctx', 'ch'), route))  16.6 us
    ppermute x14, starting transfers between devices, per_device(): tips[h][way] = lax.ppermute(tips[h][way], 'ctx', route)  13.5 us
    unnamed x42, local copies, waits for them, and re-layouts  12.9 us
    ppermute x4, starting transfers between devices, per_device(): found.append(lax.ppermute(ended[h], ('ctx', 'ch'), route))  10.7 us
    pallas_call x2, Pallas kernels, project(): pl.pallas_call(project_kernel, grid_spec=pltpu.PrefetchScalarGridSpec(num...  6.38 us
    all_to_all x1, starting transfers between devices, per_device(): packed = lax.all_to_all(packed, 'ctx', 0, 0)  5.97 us
  transfers between devices with their start and end apart: 23, of which 15 were waited for; matrix products, arithmetic and copies ran while one was open for 2% of the time, Pallas kernels for 4%

profile of v3, /device:TPU:2, one launch (start us, length us, event | category | flops | bytes accessed | tf_op | source)
XLA Modules:
  0.0 148.8 jit_solution(10275296067616001131)
XLA Ops:
  0.0 2.8 %pack.1 = bf16[8,3,256,128]{3,2,1,0:T(8,128)(2,1)} custom-call(bf16[256,1024]{1,0:T(8,128)(2,1)} %outer_ref.1, bf16[256,1024]{1,0:T(8,128)(2,1)} %inner_ref.1, bf16[256,1024]{1,0:T(8,128)(2,1)} %values_ref.1, f32[256,1024]{1,0:T(8,128)} %filters_ref.1), custom_call_target="tpu_custom_call" | custom-call | flops 262144 | bytes 4194304 | tf_op jit(solution)/shard_map/pack/pallas_call | solution.py:40
  2.8 6.0 %all-to-all-start = ((bf16[8,3,256,128]{3,2,1,0:T(8,128)(2,1)}), bf16[8,3,256,128]{3,2,1,0:T(8,128)(2,1)S(1)}, u32[]{:S(2)}, u32[]{:S(2)}) async-start(bf16[8,3,256,128]{3,2,1,0:T(8,128)(2,1)} %pack.1), calls=%async_computation | async-start | bytes 3145728 | tf_op jit(solution)/shard_map/all_to_all | solution.py:180
  8.8 36.9 %all-to-all-done.refs_0_ = bf16[8,3,256,128]{3,2,1,0:T(8,128)(2,1)S(1)} async-done(((bf16[8,3,256,128]{3,2,1,0:T(8,128)(2,1)}), bf16[8,3,256,128]{3,2,1,0:T(8,128)(2,1)S(1)}, u32[]{:S(2)}, u32[]{:S(2)}) %all-to-all-start) | async-done | bytes 1572896 | tf_op jit(solution)/shard_map/all_to_all | solution.py:180
  46.8 3.9 %convolve.1 = (bf16[1024,128]{1,0:T(8,128)(2,1)S(1)}, bf16[1024,128]{1,0:T(8,128)(2,1)S(1)}) custom-call(bf16[8,3,256,128]{3,2,1,0:T(8,128)(2,1)S(1)} %all-to-all-done.refs_0_, f32[1,128]{1,0:T(1,128)S(1)} %dynamic-slice_bitcast_fusion.refs_1_, bf16[512,512]{1,0:T(8,128)(2,1)S(1)} %copy-done.18, bf16[256,512]{1,0:T(8,128)(2,1)S(1)} %copy-done.19), custom_call_target="tpu_custom_call" | custom-call | flops 2147483648 | bytes 4194304 | tf_op jit(solution)/shard_map/convolve/pallas_call | solution.py:95
  50.7 1.5 collective-permute-start.11
  52.8 4.9 %collective-permute-done.11.refs_2_ = bf16[1024,128]{1,0:T(8,128)(2,1)S(1)} collective-permute-done((bf16[1024,128]{1,0:T(8,128)(2,1)S(1)}, bf16[1024,128]{1,0:T(8,128)(2,1)S(1)}, u32[]{:S(2)}, u32[]{:S(2)}) %collective-permute-start.11) | collective-permute-done | bytes 262176 | tf_op jit(solution)/shard_map/ppermute | solution.py:198
  57.6 1.8 %collective-permute-start.13 = (bf16[1024,128]{1,0:T(8,128)(2,1)S(1)}, bf16[1024,128]{1,0:T(8,128)(2,1)S(1)}, u32[]{:S(2)}, u32[]{:S(2)}) collective-permute-start(bf16[1024,128]{1,0:T(8,128)(2,1)S(1)} %collective-permute-done.11.refs_2_), channel_id=1, source_target_pairs={{16,8},{24,16},{28,24},{20,28},{12,20},{4,12},{0,4},{8,0},{17,9},{... | collective-permute-start | bytes 786440 | tf_op jit(solution)/shard_map/ppermute | solution.py:198
  61.1 2.9 %collective-permute-done.13.refs_4_ = bf16[1024,128]{1,0:T(8,128)(2,1)S(1)} collective-permute-done((bf16[1024,128]{1,0:T(8,128)(2,1)S(1)}, bf16[1024,128]{1,0:T(8,128)(2,1)S(1)}, u32[]{:S(2)}, u32[]{:S(2)}) %collective-permute-start.13) | collective-permute-done | bytes 262176 | tf_op jit(solution)/shard_map/ppermute | solution.py:198
  64.0 2.1 %collective-permute-start.15 = (bf16[1024,128]{1,0:T(8,128)(2,1)S(1)}, bf16[1024,128]{1,0:T(8,128)(2,1)S(1)}, u32[]{:S(2)}, u32[]{:S(2)}) collective-permute-start(bf16[1024,128]{1,0:T(8,128)(2,1)S(1)} %collective-permute-done.13.refs_4_), channel_id=1, source_target_pairs={{16,8},{24,16},{28,24},{20,28},{12,20},{4,12},{0,4},{8,0},{17,9},{... | collective-permute-start | bytes 786440 | tf_op jit(solution)/shard_map/ppermute | solution.py:198
  67.1 1.6 %collective-permute-done.refs_1_ = bf16[1024,128]{1,0:T(8,128)(2,1)S(1)} collective-permute-done((bf16[1024,128]{1,0:T(8,128)(2,1)S(1)}, bf16[1024,128]{1,0:T(8,128)(2,1)S(1)}, u32[]{:S(2)}, u32[]{:S(2)}) %collective-permute-start) | collective-permute-done | bytes 262176 | tf_op jit(solution)/shard_map/ppermute | solution.py:198
  68.9 5.4 %collective-permute-done.12.refs_3_ = bf16[1024,128]{1,0:T(8,128)(2,1)S(1)} collective-permute-done((bf16[1024,128]{1,0:T(8,128)(2,1)S(1)}, bf16[1024,128]{1,0:T(8,128)(2,1)S(1)}, u32[]{:S(2)}, u32[]{:S(2)}) %collective-permute-start.12) | collective-permute-done | bytes 262176 | tf_op jit(solution)/shard_map/ppermute | solution.py:198
  75.0 2.0 %collective-permute-start.16 = (bf16[1024,128]{1,0:T(8,128)(2,1)S(1)}, bf16[1024,128]{1,0:T(8,128)(2,1)S(1)}, u32[]{:S(2)}, u32[]{:S(2)}) collective-permute-start(bf16[1024,128]{1,0:T(8,128)(2,1)S(1)} %collective-permute-done.15.refs_6_), channel_id=1, source_target_pairs={{16,8},{24,16},{28,24},{20,28},{12,20},{4,12},{0,4},{8,0},{17,9},{... | collective-permute-start | bytes 786440 | tf_op jit(solution)/shard_map/ppermute | solution.py:198
  77.7 1.4 collective-permute-done.1.refs_2_
  79.2 1.7 %collective-permute-start.3 = (bf16[1024,128]{1,0:T(8,128)(2,1)S(1)}, bf16[1024,128]{1,0:T(8,128)(2,1)}, u32[]{:S(2)}, u32[]{:S(2)}) collective-permute-start(bf16[1024,128]{1,0:T(8,128)(2,1)S(1)} %collective-permute-done.1.refs_2_), channel_id=1, source_target_pairs={{16,8},{24,16},{28,24},{20,28},{12,20},{4,12},{0,4},{8,0},{17,9},{... | collective-permute-start | bytes 786440 | tf_op jit(solution)/shard_map/ppermute | solution.py:198
  81.3 3.8 %collective-permute-done.14.refs_5_ = bf16[1024,128]{1,0:T(8,128)(2,1)S(1)} collective-permute-done((bf16[1024,128]{1,0:T(8,128)(2,1)S(1)}, bf16[1024,128]{1,0:T(8,128)(2,1)S(1)}, u32[]{:S(2)}, u32[]{:S(2)}) %collective-permute-start.14) | collective-permute-done | bytes 262176 | tf_op jit(solution)/shard_map/ppermute | solution.py:198
  92.3 2.5 %project.3 = (bf16[512,512]{1,0:T(8,128)(2,1)S(1)}, bf16[512,512]{1,0:T(8,128)(2,1)S(1)}) custom-call(s32[2]{0:T(128)S(1)} %pad_add_fusion.here_ref, s32[64]{0:T(128)S(1)} %copy-done.20, bf16[1024,128]{1,0:T(8,128)(2,1)S(1)} %get-tuple-element.14.refs_0_, bf16[1024,128]{1,0:T(8,128)(2,1)S(1)} %copy-done.7, ...), custom_call_target="tpu_custom_call" | custom-call | flops 1073741824 | bytes 4194304 | tf_op jit(solution)/shard_map/project/pallas_call | solution.py:137
  95.0 2.0 %collective-permute-start.6 = (bf16[1024,128]{1,0:T(8,128)(2,1)}, bf16[1024,128]{1,0:T(8,128)(2,1)S(1)}, u32[]{:S(2)}, u32[]{:S(2)}) collective-permute-start(bf16[1024,128]{1,0:T(8,128)(2,1)} %collective-permute-done.4.refs_5_), channel_id=1, source_target_pairs={{8,16},{16,24},{24,28},{28,20},{20,12},{12,4},{4,0},{0,8},{9,17},{... | collective-permute-start | bytes 786440 | tf_op jit(solution)/shard_map/ppermute | solution.py:198
  97.0 6.8 %collective-permute-done.5.refs_6_ = bf16[1024,128]{1,0:T(8,128)(2,1)S(1)} collective-permute-done((bf16[1024,128]{1,0:T(8,128)(2,1)}, bf16[1024,128]{1,0:T(8,128)(2,1)S(1)}, u32[]{:S(2)}, u32[]{:S(2)}) %collective-permute-start.5) | collective-permute-done | bytes 262176 | tf_op jit(solution)/shard_map/ppermute | solution.py:198
  105.8 3.9 %project.2 = (bf16[512,512]{1,0:T(8,128)(2,1)S(1)}, bf16[512,512]{1,0:T(8,128)(2,1)S(1)}) custom-call(s32[2]{0:T(128)S(1)} %pad_add_fusion.here_ref, s32[64]{0:T(128)S(1)} %copy-done.20, bf16[1024,128]{1,0:T(8,128)(2,1)S(1)} %get-tuple-element.11.refs_0_, bf16[1024,128]{1,0:T(8,128)(2,1)S(1)} %copy-done.3, bf16[1024,128]{1,0:T(8,128)(2,1)S(1)} %copy-done.5, ...), custom_call_target="tpu_custom_call" | custom-call | flops 1073741824 | bytes 4194304 | tf_op jit(solution)/shard_map/project/pallas_call | solution.py:137
  114.5 5.8 %collective-permute-done.18 = bf16[1,256,512]{2,1,0:T(8,128)(2,1)S(1)} collective-permute-done((bf16[1,256,512]{2,1,0:T(8,128)(2,1)S(1)}, bf16[1,256,512]{2,1,0:T(8,128)(2,1)S(1)}, u32[]{:S(2)}, u32[]{:S(2)}) %collective-permute-start.18) | collective-permute-done | bytes 262176 | tf_op jit(solution)/shard_map/ppermute | solution.py:216
  120.3 4.9 %collective-permute-start.19 = (bf16[256,512]{1,0:T(8,128)(2,1)S(1)}, bf16[256,512]{1,0:T(8,128)(2,1)S(1)}, u32[]{:S(2)}, u32[]{:S(2)}) collective-permute-start(bf16[256,512]{1,0:T(8,128)(2,1)S(1)} %fusion.5), channel_id=1, source_target_pairs={{0,8},{1,24},{2,12},{3,28},{8,9},{9,25},{10,13},{11,29},{16,10},{1... | collective-permute-start | bytes 786440 | tf_op jit(solution)/shard_map/ppermute | solution.py:230
  125.5 3.7 %collective-permute-start.9 = (bf16[256,512]{1,0:T(8,128)(2,1)S(1)}, bf16[256,512]{1,0:T(8,128)(2,1)S(1)}, u32[]{:S(2)}, u32[]{:S(2)}) collective-permute-start(bf16[256,512]{1,0:T(8,128)(2,1)S(1)} %fusion.4), channel_id=1, source_target_pairs={{0,0},{1,16},{2,4},{3,20},{8,1},{9,17},{10,5},{11,21},{16,2},{17,1... | collective-permute-start | bytes 786440 | tf_op jit(solution)/shard_map/ppermute | solution.py:230
  131.5 7.3 %collective-permute-done.9 = bf16[256,512]{1,0:T(8,128)(2,1)S(1)} collective-permute-done((bf16[256,512]{1,0:T(8,128)(2,1)S(1)}, bf16[256,512]{1,0:T(8,128)(2,1)S(1)}, u32[]{:S(2)}, u32[]{:S(2)}) %collective-permute-start.9) | collective-permute-done | bytes 262176 | tf_op jit(solution)/shard_map/ppermute | solution.py:230
  138.9 9.0 %collective-permute-done.20 = bf16[256,512]{1,0:T(8,128)(2,1)S(1)} collective-permute-done((bf16[256,512]{1,0:T(8,128)(2,1)S(1)}, bf16[256,512]{1,0:T(8,128)(2,1)S(1)}, u32[]{:S(2)}, u32[]{:S(2)}) %collective-permute-start.20) | collective-permute-done | bytes 262176 | tf_op jit(solution)/shard_map/ppermute | solution.py:230
  (79 shorter events, 23.8 us)
Async XLA Ops:
  2.8 43.0 %all-to-all-start = ((bf16[8,3,256,128]{3,2,1,0:T(8,128)(2,1)}), bf16[8,3,256,128]{3,2,1,0:T(8,128)(2,1)S(1)}, u32[]{:S(2)}, u32[]{:S(2)}) async-start(bf16[8,3,256,128]{3,2,1,0:T(8,128)(2,1)} %pack.1), calls=%async_computation | async-start | bytes 3145728 | tf_op jit(solution)/shard_map/all_to_all | solution.py:180
  8.8 77.8 %copy-start.1 = (bf16[1024,512]{1,0:T(8,128)(2,1)S(1)}, bf16[1024,512]{1,0:T(8,128)(2,1)}, u32[]{:S(2)}) copy-start(bf16[1024,512]{1,0:T(8,128)(2,1)} %param.15) | copy-start | bytes 3145732
  50.7 7.0 %collective-permute-start.11 = (bf16[1024,128]{1,0:T(8,128)(2,1)S(1)}, bf16[1024,128]{1,0:T(8,128)(2,1)S(1)}, u32[]{:S(2)}, u32[]{:S(2)}) collective-permute-start(bf16[1024,128]{1,0:T(8,128)(2,1)S(1)} %get-tuple-element.14.refs_0_), channel_id=1, source_target_pairs={{16,8},{24,16},{28,24},{20,28},{12,20},{4,12},{0,4},{8,0},{17,9},{... | collective-permute-start | bytes 786440 | tf_op jit(solution)/shard_map/ppermute | solution.py:198
  52.2 7.5 %collective-permute-start.10 = (bf16[1024,128]{1,0:T(8,128)(2,1)S(1)}, bf16[1024,128]{1,0:T(8,128)(2,1)S(1)}, u32[]{:S(2)}, u32[]{:S(2)}) collective-permute-start(bf16[1024,128]{1,0:T(8,128)(2,1)S(1)} %get-tuple-element.14.refs_0_), channel_id=1, source_target_pairs={{8,16},{16,24},{24,28},{28,20},{20,12},{12,4},{4,0},{0,8},{9,17},{... | collective-permute-start | bytes 786440 | tf_op jit(solution)/shard_map/ppermute | solution.py:198
  57.6 6.4 %collective-permute-start.13 = (bf16[1024,128]{1,0:T(8,128)(2,1)S(1)}, bf16[1024,128]{1,0:T(8,128)(2,1)S(1)}, u32[]{:S(2)}, u32[]{:S(2)}) collective-permute-start(bf16[1024,128]{1,0:T(8,128)(2,1)S(1)} %collective-permute-done.11.refs_2_), channel_id=1, source_target_pairs={{16,8},{24,16},{28,24},{20,28},{12,20},{4,12},{0,4},{8,0},{17,9},{... | collective-permute-start | bytes 786440 | tf_op jit(solution)/shard_map/ppermute | solution.py:198
  59.4 9.2 %collective-permute-start = (bf16[1024,128]{1,0:T(8,128)(2,1)S(1)}, bf16[1024,128]{1,0:T(8,128)(2,1)S(1)}, u32[]{:S(2)}, u32[]{:S(2)}) collective-permute-start(bf16[1024,128]{1,0:T(8,128)(2,1)S(1)} %get-tuple-element.11.refs_0_), channel_id=1, source_target_pairs={{8,16},{16,24},{24,28},{28,20},{20,12},{12,4},{4,0},{0,8},{9,17},{... | collective-permute-start | bytes 786440 | tf_op jit(solution)/shard_map/ppermute | solution.py:198
  59.7 14.6 %collective-permute-start.12 = (bf16[1024,128]{1,0:T(8,128)(2,1)S(1)}, bf16[1024,128]{1,0:T(8,128)(2,1)S(1)}, u32[]{:S(2)}, u32[]{:S(2)}) collective-permute-start(bf16[1024,128]{1,0:T(8,128)(2,1)S(1)} %collective-permute-done.10.refs_1_), channel_id=1, source_target_pairs={{8,16},{16,24},{24,28},{28,20},{20,12},{12,4},{4,0},{0,8},{9,17},{... | collective-permute-start | bytes 786440 | tf_op jit(solution)/shard_map/ppermute | solution.py:198
  64.0 11.0 %collective-permute-start.15 = (bf16[1024,128]{1,0:T(8,128)(2,1)S(1)}, bf16[1024,128]{1,0:T(8,128)(2,1)S(1)}, u32[]{:S(2)}, u32[]{:S(2)}) collective-permute-start(bf16[1024,128]{1,0:T(8,128)(2,1)S(1)} %collective-permute-done.13.refs_4_), channel_id=1, source_target_pairs={{16,8},{24,16},{28,24},{20,28},{12,20},{4,12},{0,4},{8,0},{17,9},{... | collective-permute-start | bytes 786440 | tf_op jit(solution)/shard_map/ppermute | solution.py:198
  66.9 12.3 %collective-permute-start.1 = (bf16[1024,128]{1,0:T(8,128)(2,1)S(1)}, bf16[1024,128]{1,0:T(8,128)(2,1)S(1)}, u32[]{:S(2)}, u32[]{:S(2)}) collective-permute-start(bf16[1024,128]{1,0:T(8,128)(2,1)S(1)} %get-tuple-element.11.refs_0_), channel_id=1, source_target_pairs={{16,8},{24,16},{28,24},{20,28},{12,20},{4,12},{0,4},{8,0},{17,9},{... | collective-permute-start | bytes 786440 | tf_op jit(solution)/shard_map/ppermute | solution.py:198
  68.7 12.2 %collective-permute-start.2 = (bf16[1024,128]{1,0:T(8,128)(2,1)S(1)}, bf16[1024,128]{1,0:T(8,128)(2,1)}, u32[]{:S(2)}, u32[]{:S(2)}) collective-permute-start(bf16[1024,128]{1,0:T(8,128)(2,1)S(1)} %collective-permute-done.refs_1_), channel_id=1, source_target_pairs={{8,16},{16,24},{24,28},{28,20},{20,12},{12,4},{4,0},{0,8},{9,17},{... | collective-permute-start | bytes 786440 | tf_op jit(solution)/shard_map/ppermute | solution.py:198
  74.3 10.9 %collective-permute-start.14 = (bf16[1024,128]{1,0:T(8,128)(2,1)S(1)}, bf16[1024,128]{1,0:T(8,128)(2,1)S(1)}, u32[]{:S(2)}, u32[]{:S(2)}) collective-permute-start(bf16[1024,128]{1,0:T(8,128)(2,1)S(1)} %collective-permute-done.12.refs_3_), channel_id=1, source_target_pairs={{8,16},{16,24},{24,28},{28,20},{20,12},{12,4},{4,0},{0,8},{9,17},{... | collective-permute-start | bytes 786440 | tf_op jit(solution)/shard_map/ppermute | solution.py:198
  75.0 10.9 %collective-permute-start.16 = (bf16[1024,128]{1,0:T(8,128)(2,1)S(1)}, bf16[1024,128]{1,0:T(8,128)(2,1)S(1)}, u32[]{:S(2)}, u32[]{:S(2)}) collective-permute-start(bf16[1024,128]{1,0:T(8,128)(2,1)S(1)} %collective-permute-done.15.refs_6_), channel_id=1, source_target_pairs={{16,8},{24,16},{28,24},{20,28},{12,20},{4,12},{0,4},{8,0},{17,9},{... | collective-permute-start | bytes 786440 | tf_op jit(solution)/shard_map/ppermute | solution.py:198
  79.2 15.7 %collective-permute-start.3 = (bf16[1024,128]{1,0:T(8,128)(2,1)S(1)}, bf16[1024,128]{1,0:T(8,128)(2,1)}, u32[]{:S(2)}, u32[]{:S(2)}) collective-permute-start(bf16[1024,128]{1,0:T(8,128)(2,1)S(1)} %collective-permute-done.1.refs_2_), channel_id=1, source_target_pairs={{16,8},{24,16},{28,24},{20,28},{12,20},{4,12},{0,4},{8,0},{17,9},{... | collective-permute-start | bytes 786440 | tf_op jit(solution)/shard_map/ppermute | solution.py:198
  80.9 14.1 %collective-permute-start.4 = (bf16[1024,128]{1,0:T(8,128)(2,1)}, bf16[1024,128]{1,0:T(8,128)(2,1)}, u32[]{:S(2)}, u32[]{:S(2)}) collective-permute-start(bf16[1024,128]{1,0:T(8,128)(2,1)} %collective-permute-done.2.refs_3_), channel_id=1, source_target_pairs={{8,16},{16,24},{24,28},{28,20},{20,12},{12,4},{4,0},{0,8},{9,17},{... | collective-permute-start | bytes 786440 | tf_op jit(solution)/shard_map/ppermute | solution.py:198
  94.8 15.0 %collective-permute-start.17 = (bf16[512,512]{1,0:T(8,128)(2,1)S(1)}, bf16[512,512]{1,0:T(8,128)(2,1)}, u32[]{:S(2)}, u32[]{:S(2)}) collective-permute-start(bf16[512,512]{1,0:T(8,128)(2,1)S(1)} %get-tuple-element.16), channel_id=1, source_target_pairs={{0,1},{1,0},{2,3},{3,2},{4,5},{5,4},{6,7},{7,6},{8,9},{9,8},{10,11... | collective-permute-start | bytes 1572872 | tf_op jit(solution)/shard_map/ppermute | solution.py:208
  94.9 8.9 %collective-permute-start.5 = (bf16[1024,128]{1,0:T(8,128)(2,1)}, bf16[1024,128]{1,0:T(8,128)(2,1)S(1)}, u32[]{:S(2)}, u32[]{:S(2)}) collective-permute-start(bf16[1024,128]{1,0:T(8,128)(2,1)} %collective-permute-done.3.refs_4_), channel_id=1, source_target_pairs={{16,8},{24,16},{28,24},{20,28},{12,20},{4,12},{0,4},{8,0},{17,9},{... | collective-permute-start | bytes 786440 | tf_op jit(solution)/shard_map/ppermute | solution.py:198
  95.0 8.9 %collective-permute-start.6 = (bf16[1024,128]{1,0:T(8,128)(2,1)}, bf16[1024,128]{1,0:T(8,128)(2,1)S(1)}, u32[]{:S(2)}, u32[]{:S(2)}) collective-permute-start(bf16[1024,128]{1,0:T(8,128)(2,1)} %collective-permute-done.4.refs_5_), channel_id=1, source_target_pairs={{8,16},{16,24},{24,28},{28,20},{20,12},{12,4},{4,0},{0,8},{9,17},{... | collective-permute-start | bytes 786440 | tf_op jit(solution)/shard_map/ppermute | solution.py:198
  109.7 2.1 %collective-permute-start.7 = (bf16[512,512]{1,0:T(8,128)(2,1)S(1)}, bf16[512,512]{1,0:T(8,128)(2,1)}, u32[]{:S(2)}, u32[]{:S(2)}) collective-permute-start(bf16[512,512]{1,0:T(8,128)(2,1)S(1)} %get-tuple-element.13), channel_id=1, source_target_pairs={{0,1},{1,0},{2,3},{3,2},{4,5},{5,4},{6,7},{7,6},{8,9},{9,8},{10,11... | collective-permute-start | bytes 1572872 | tf_op jit(solution)/shard_map/ppermute | solution.py:208
  111.1 9.2 %collective-permute-start.18 = (bf16[1,256,512]{2,1,0:T(8,128)(2,1)S(1)}, bf16[1,256,512]{2,1,0:T(8,128)(2,1)S(1)}, u32[]{:S(2)}, u32[]{:S(2)}) collective-permute-start(bf16[1,256,512]{2,1,0:T(8,128)(2,1)S(1)} %fusion.3), channel_id=1, source_target_pairs={{0,2},{1,3},{2,0},{3,1},{4,6},{5,7},{6,4},{7,5},{8,10},{9,11},{10,... | collective-permute-start | bytes 786440 | tf_op jit(solution)/shard_map/ppermute | solution.py:216
  113.0 12.4 %collective-permute-start.8 = (bf16[1,256,512]{2,1,0:T(8,128)(2,1)S(1)}, bf16[1,256,512]{2,1,0:T(8,128)(2,1)S(1)}, u32[]{:S(2)}, u32[]{:S(2)}) collective-permute-start(bf16[1,256,512]{2,1,0:T(8,128)(2,1)S(1)} %fusion.2), channel_id=1, source_target_pairs={{0,2},{1,3},{2,0},{3,1},{4,6},{5,7},{6,4},{7,5},{8,10},{9,11},{10,... | collective-permute-start | bytes 786440 | tf_op jit(solution)/shard_map/ppermute | solution.py:216
  120.3 11.2 %collective-permute-start.19 = (bf16[256,512]{1,0:T(8,128)(2,1)S(1)}, bf16[256,512]{1,0:T(8,128)(2,1)S(1)}, u32[]{:S(2)}, u32[]{:S(2)}) collective-permute-start(bf16[256,512]{1,0:T(8,128)(2,1)S(1)} %fusion.5), channel_id=1, source_target_pairs={{0,8},{1,24},{2,12},{3,28},{8,9},{9,25},{10,13},{11,29},{16,10},{1... | collective-permute-start | bytes 786440 | tf_op jit(solution)/shard_map/ppermute | solution.py:230
  125.5 13.4 %collective-permute-start.9 = (bf16[256,512]{1,0:T(8,128)(2,1)S(1)}, bf16[256,512]{1,0:T(8,128)(2,1)S(1)}, u32[]{:S(2)}, u32[]{:S(2)}) collective-permute-start(bf16[256,512]{1,0:T(8,128)(2,1)S(1)} %fusion.4), channel_id=1, source_target_pairs={{0,0},{1,16},{2,4},{3,20},{8,1},{9,17},{10,5},{11,21},{16,2},{17,1... | collective-permute-start | bytes 786440 | tf_op jit(solution)/shard_map/ppermute | solution.py:230
  129.2 9.6 %collective-permute-start.21 = (bf16[256,512]{1,0:T(8,128)(2,1)S(1)}, bf16[256,512]{1,0:T(8,128)(2,1)S(1)}, u32[]{:S(2)}, u32[]{:S(2)}) collective-permute-start(bf16[256,512]{1,0:T(8,128)(2,1)S(1)} %fusion.5), channel_id=1, source_target_pairs={{4,8},{5,24},{6,12},{7,28},{12,9},{13,25},{14,13},{15,29},{20,10},... | collective-permute-start | bytes 786440 | tf_op jit(solution)/shard_map/ppermute | solution.py:230
  129.9 18.0 %collective-permute-start.20 = (bf16[256,512]{1,0:T(8,128)(2,1)S(1)}, bf16[256,512]{1,0:T(8,128)(2,1)S(1)}, u32[]{:S(2)}, u32[]{:S(2)}) collective-permute-start(bf16[256,512]{1,0:T(8,128)(2,1)S(1)} %fusion.4), channel_id=1, source_target_pairs={{4,0},{5,16},{6,4},{7,20},{12,1},{13,17},{14,5},{15,21},{20,2},{21... | collective-permute-start | bytes 786440 | tf_op jit(solution)/shard_map/ppermute | solution.py:230
  (20 other events, 146.2 us)

commit v4 on v3

--- a/solution.py
+++ b/solution.py
@@ -147,12 +147,8 @@
             ],
         ),
         out_shape=[part, part],
-        compiler_params=pltpu.CompilerParams(vmem_limit_bytes=10 * MIB),
-        cost_estimate=pl.CostEstimate(
-            flops=2 * count * block * n * chans * columns,
-            bytes_accessed=4 * MIB,
-            transcendentals=0,
-        ),
+        compiler_params=pltpu.CompilerParams(vmem_limit_bytes=60 * MIB),
+        cost_estimate=pl.CostEstimate(flops=0, bytes_accessed=0, transcendentals=0),
         name="project",
     )(here, table, *pieces, w_out.reshape(n, chans, columns))
 
@@ -191,7 +187,12 @@
     pieces = [[mix] for mix in mixes]
     offsets = [[0], [0]]
     tips = [[mix, mix] for mix in mixes]
+    late = []
     for s in range(n // 2):
+        if s >= 2:
+            tied = lax.optimization_barrier((*tips[0], *late[s - 1]))
+            tips[0] = list(tied[:2])
+        late.append(list(tips[1]))
         for h in range(2):
             for way, route in enumerate((onward, back)):
                 if s < hops[h][way]:
@@ -201,11 +202,15 @@
 
     half = m // 2
     swap = [(d, d ^ 1) for d in range(m)]
-    ended = []
+    placed = [[], []]
+    gate = []
     for h in range(2):
+        ahead = late[-1] if h == 0 else gate
+        pieces[h][-1], *_ = lax.optimization_barrier((pieces[h][-1], *ahead))
         owners = np.array([[ring[(spot[a] + o) % n] for o in offsets[h]] for a in range(n)], np.int32)
         keep, give = project(pieces[h], here, jnp.asarray(owners.reshape(-1)), w_out, block)
         got = lax.ppermute(give, "ch", swap)
+        got, *_ = lax.optimization_barrier((got, pieces[1][-1] if h == 0 else ended))
         kept = (keep.astype(F32) + got.astype(F32)).reshape(half, block, -1)
         bit = 1
         while bit < half:
@@ -213,23 +218,23 @@
             split = kept.reshape((kept.shape[0] // 2, 2) + kept.shape[1:])
             keep = lax.dynamic_index_in_dim(split, mine, 1, keepdims=False)
             give = lax.dynamic_index_in_dim(split, 1 - mine, 1, keepdims=False).astype(BF16)
+            gate = [give]
             got = lax.ppermute(give, "ch", [(d, d ^ (2 * bit)) for d in range(m)])
+            if h:
+                got, *_ = lax.optimization_barrier((got, *placed[0]))
             kept = keep + got.astype(F32)
             bit *= 2
-        ended.append(kept[0].astype(BF16))
-
-    columns = []
-    for c in range(q):
-        found = []
-        for h in range(2):
+        ended = kept[0].astype(BF16)
+        for c in range(q):
             route = []
             for a in range(c, n, q):
                 for b in range(m):
                     r = of[h][(b % 2) * half + b // 2]
                     route.append((a * m + b, r * m + a // q))
-            found.append(lax.ppermute(ended[h], ("ctx", "ch"), route))
-        columns.append(jnp.where((j // across) % 2 == 0, found[0], found[1]))
-    return jnp.concatenate(columns, axis=1)
+            placed[h].append(lax.ppermute(ended, ("ctx", "ch"), route))
+
+    even = (j // across) % 2 == 0
+    return jnp.concatenate([jnp.where(even, a, b) for a, b in zip(*placed)], axis=1)
 
 
 def solution(mesh):

time: 150 us -> 154 us (1.027)
  the two profiles are of different devices: /device:TPU:2 before, /device:TPU:10 now
where the time goes in v4:
time: 154 us; the launch traced here: 153 us
  waiting for transfers between devices  95.6 us (62%)
  starting transfers between devices  33.9 us (22%)
  Pallas kernels  18.3 us (12%)
  other arithmetic  4.21 us (3%)
    all_to_all x1, waiting for transfers between devices, per_device(): packed = lax.all_to_all(packed, 'ctx', 0, 0)  34.2 us
    ppermute x14, waiting for transfers between devices, per_device(): tips[h][way] = lax.ppermute(tips[h][way], 'ctx', route)  33.6 us
    ppermute x4, waiting for transfers between devices, per_device(): placed[h].append(lax.ppermute(ended, ('ctx', 'ch'), route))  19 us
    ppermute x14, starting transfers between devices, per_device(): tips[h][way] = lax.ppermute(tips[h][way], 'ctx', route)  15.8 us
    pallas_call x2, Pallas kernels, project(): pl.pallas_call(project_kernel, grid_spec=pltpu.PrefetchScalarGridSpec(num...  11.6 us
    ppermute x4, starting transfers between devices, per_device(): placed[h].append(lax.ppermute(ended, ('ctx', 'ch'), route))  10.9 us
    ppermute x2, waiting for transfers between devices, per_device(): got = lax.ppermute(give, 'ch', [(d, d ^ 2 * bit) for d in range(m)])  8.73 us
    all_to_all x1, starting transfers between devices, per_device(): packed = lax.all_to_all(packed, 'ctx', 0, 0)  6.42 us
  transfers between devices with their start and end apart: 23, of which 18 were waited for; matrix products, arithmetic and copies ran while one was open for 1% of the time, Pallas kernels for 0%

profile of v4, /device:TPU:10, one launch (start us, length us, event | category | flops | bytes accessed | tf_op | source)
XLA Modules:
  0.0 153.1 jit_solution(581343260877719656)
XLA Ops:
  0.0 2.8 %pack.1 = bf16[8,3,256,128]{3,2,1,0:T(8,128)(2,1)} custom-call(bf16[256,1024]{1,0:T(8,128)(2,1)} %outer_ref.1, bf16[256,1024]{1,0:T(8,128)(2,1)} %inner_ref.1, bf16[256,1024]{1,0:T(8,128)(2,1)} %values_ref.1, f32[256,1024]{1,0:T(8,128)} %filters_ref.1), custom_call_target="tpu_custom_call" | custom-call | flops 262144 | bytes 4194304 | tf_op jit(solution)/shard_map/pack/pallas_call | solution.py:40
  2.8 6.4 %all-to-all-start = ((bf16[8,3,256,128]{3,2,1,0:T(8,128)(2,1)}), bf16[8,3,256,128]{3,2,1,0:T(8,128)(2,1)S(1)}, u32[]{:S(2)}, u32[]{:S(2)}) async-start(bf16[8,3,256,128]{3,2,1,0:T(8,128)(2,1)} %pack.1), calls=%async_computation | async-start | bytes 3145728 | tf_op jit(solution)/shard_map/all_to_all | solution.py:176
  9.3 34.2 %all-to-all-done.refs_0_ = bf16[8,3,256,128]{3,2,1,0:T(8,128)(2,1)S(1)} async-done(((bf16[8,3,256,128]{3,2,1,0:T(8,128)(2,1)}), bf16[8,3,256,128]{3,2,1,0:T(8,128)(2,1)S(1)}, u32[]{:S(2)}, u32[]{:S(2)}) %all-to-all-start) | async-done | bytes 1572896 | tf_op jit(solution)/shard_map/all_to_all | solution.py:176
  43.5 3.9 %convolve.1 = (bf16[1024,128]{1,0:T(8,128)(2,1)S(1)}, bf16[1024,128]{1,0:T(8,128)(2,1)S(1)}) custom-call(bf16[8,3,256,128]{3,2,1,0:T(8,128)(2,1)S(1)} %all-to-all-done.refs_0_, f32[1,128]{1,0:T(1,128)S(1)} %dynamic-slice_bitcast_fusion.refs_1_, bf16[512,512]{1,0:T(8,128)(2,1)S(1)} %copy-done.3, bf16[256,512]{1,0:T(8,128)(2,1)S(1)} %copy-done.4), custom_call_target="tpu_custom_call" | custom-call | flops 2147483648 | bytes 4194304 | tf_op jit(solution)/shard_map/convolve/pallas_call | solution.py:95
  48.4 1.9 %collective-permute-start.1 = (bf16[1024,128]{1,0:T(8,128)(2,1)S(1)}, bf16[1024,128]{1,0:T(8,128)(2,1)S(1)}, u32[]{:S(2)}, u32[]{:S(2)}) collective-permute-start(bf16[1024,128]{1,0:T(8,128)(2,1)S(1)} %get-tuple-element.19.refs_0_), channel_id=1, source_target_pairs={{16,8},{24,16},{28,24},{20,28},{12,20},{4,12},{0,4},{8,0},{17,9},{... | collective-permute-start | bytes 786440 | tf_op jit(solution)/shard_map/ppermute | solution.py:199
  52.3 5.1 %collective-permute-done.refs_1_ = bf16[1024,128]{1,0:T(8,128)(2,1)S(1)} collective-permute-done((bf16[1024,128]{1,0:T(8,128)(2,1)S(1)}, bf16[1024,128]{1,0:T(8,128)(2,1)S(1)}, u32[]{:S(2)}, u32[]{:S(2)}) %collective-permute-start) | collective-permute-done | bytes 262176 | tf_op jit(solution)/shard_map/ppermute | solution.py:199
  59.5 3.5 %collective-permute-done.4.refs_1_ = bf16[1024,128]{1,0:T(8,128)(2,1)S(1)} collective-permute-done((bf16[1024,128]{1,0:T(8,128)(2,1)S(1)}, bf16[1024,128]{1,0:T(8,128)(2,1)S(1)}, u32[]{:S(2)}, u32[]{:S(2)}) %collective-permute-start.4) | collective-permute-done | bytes 262176 | tf_op jit(solution)/shard_map/ppermute | solution.py:199
  65.1 3.5 %collective-permute-done.2.refs_3_ = bf16[1024,128]{1,0:T(8,128)(2,1)S(1)} collective-permute-done((bf16[1024,128]{1,0:T(8,128)(2,1)S(1)}, bf16[1024,128]{1,0:T(8,128)(2,1)S(1)}, u32[]{:S(2)}, u32[]{:S(2)}) %collective-permute-start.2) | collective-permute-done | bytes 262176 | tf_op jit(solution)/shard_map/ppermute | solution.py:199
  69.7 2.1 %collective-permute-start.6 = (bf16[1024,128]{1,0:T(8,128)(2,1)S(1)}, bf16[1024,128]{1,0:T(8,128)(2,1)S(1)}, u32[]{:S(2)}, u32[]{:S(2)}) collective-permute-start(bf16[1024,128]{1,0:T(8,128)(2,1)S(1)} %collective-permute-done.2.refs_3_), channel_id=1, source_target_pairs={{8,16},{16,24},{24,28},{28,20},{20,12},{12,4},{4,0},{0,8},{9,17},{... | collective-permute-start | bytes 786440 | tf_op jit(solution)/shard_map/ppermute | solution.py:199
  71.7 3.5 %collective-permute-done.9.refs_4_ = bf16[1024,128]{1,0:T(8,128)(2,1)S(1)} collective-permute-done((bf16[1024,128]{1,0:T(8,128)(2,1)S(1)}, bf16[1024,128]{1,0:T(8,128)(2,1)S(1)}, u32[]{:S(2)}, u32[]{:S(2)}) %collective-permute-start.9) | collective-permute-done | bytes 262176 | tf_op jit(solution)/shard_map/ppermute | solution.py:199
  77.4 2.4 %collective-permute-done.6.refs_5_ = bf16[1024,128]{1,0:T(8,128)(2,1)S(1)} collective-permute-done((bf16[1024,128]{1,0:T(8,128)(2,1)S(1)}, bf16[1024,128]{1,0:T(8,128)(2,1)S(1)}, u32[]{:S(2)}, u32[]{:S(2)}) %collective-permute-start.6) | collective-permute-done | bytes 262176 | tf_op jit(solution)/shard_map/ppermute | solution.py:199
  81.7 2.0 %collective-permute-start.10 = (bf16[1024,128]{1,0:T(8,128)(2,1)S(1)}, bf16[1024,128]{1,0:T(8,128)(2,1)}, u32[]{:S(2)}, u32[]{:S(2)}) collective-permute-start(bf16[1024,128]{1,0:T(8,128)(2,1)S(1)} %collective-permute-done.6.refs_5_), channel_id=1, source_target_pairs={{8,16},{16,24},{24,28},{28,20},{20,12},{12,4},{4,0},{0,8},{9,17},{... | collective-permute-start | bytes 786440 | tf_op jit(solution)/shard_map/ppermute | solution.py:199
  85.6 3.9 %collective-permute-done.10.refs_7_ = bf16[1024,128]{1,0:T(8,128)(2,1)} collective-permute-done((bf16[1024,128]{1,0:T(8,128)(2,1)S(1)}, bf16[1024,128]{1,0:T(8,128)(2,1)}, u32[]{:S(2)}, u32[]{:S(2)}) %collective-permute-start.10) | collective-permute-done | bytes 262176 | tf_op jit(solution)/shard_map/ppermute | solution.py:199
  89.5 5.8 %project.2 = (bf16[512,512]{1,0:T(8,128)(2,1)}, bf16[512,512]{1,0:T(8,128)(2,1)}) custom-call(s32[2]{0:T(128)} %pad_add_fusion.here_ref, s32[64]{0:T(128)} %constant.84.clone.table_ref, bf16[1024,128]{1,0:T(8,128)(2,1)} %copy-done.2, bf16[1024,128]{1,0:T(8,128)(2,1)} %copy-done.11, bf16[1024,128]{1,0:T(8,128)(2,1)} %copy-done.12, ...), custom_call_target="tpu_custom_call" | custom-call | tf_op jit(solution)/shard_map/project/pallas_call | solution.py:137
  95.5 1.5 collective-permute-start.14
  97.0 7.2 %collective-permute-done.14.refs_7_ = bf16[1024,128]{1,0:T(8,128)(2,1)S(1)} collective-permute-done((bf16[1024,128]{1,0:T(8,128)(2,1)S(1)}, bf16[1024,128]{1,0:T(8,128)(2,1)S(1)}, u32[]{:S(2)}, u32[]{:S(2)}) %collective-permute-start.14) | collective-permute-done | bytes 262176 | tf_op jit(solution)/shard_map/ppermute | solution.py:199
  104.2 1.3 convert_add_fusion.1
  105.5 5.8 %project.3 = (bf16[512,512]{1,0:T(8,128)(2,1)}, bf16[512,512]{1,0:T(8,128)(2,1)}) custom-call(s32[2]{0:T(128)} %pad_add_fusion.here_ref, s32[64]{0:T(128)} %constant.84.clone.table_ref, bf16[1024,128]{1,0:T(8,128)(2,1)} %copy-done.1, bf16[1024,128]{1,0:T(8,128)(2,1)} %copy-done.5, bf16[1024,128]{1,0:T(8,128)(2,1)} %copy-done.6, bf16[1024,128]{1,0:T(8,128)(2,1)} %copy-done.7, ...), custom_call_target="tpu_custom_call" | custom-call | tf_op jit(solution)/shard_map/project/pallas_call | solution.py:137
  112.0 8.1 %collective-permute-done.15 = bf16[1,256,512]{2,1,0:T(8,128)(2,1)S(1)} collective-permute-done((bf16[1,256,512]{2,1,0:T(8,128)(2,1)S(1)}, bf16[1,256,512]{2,1,0:T(8,128)(2,1)S(1)}, u32[]{:S(2)}, u32[]{:S(2)}) %collective-permute-start.15) | collective-permute-done | bytes 262176 | tf_op jit(solution)/shard_map/ppermute | solution.py:222
  120.2 3.8 %collective-permute-start.16 = (bf16[256,512]{1,0:T(8,128)(2,1)S(1)}, bf16[256,512]{1,0:T(8,128)(2,1)S(1)}, u32[]{:S(2)}, u32[]{:S(2)}) collective-permute-start(bf16[256,512]{1,0:T(8,128)(2,1)S(1)} %fusion.4), channel_id=1, source_target_pairs={{0,0},{1,16},{2,4},{3,20},{8,1},{9,17},{10,5},{11,21},{16,2},{17,1... | collective-permute-start | bytes 786440 | tf_op jit(solution)/shard_map/ppermute | solution.py:234
  126.0 7.5 %collective-permute-done.16 = bf16[256,512]{1,0:T(8,128)(2,1)S(1)} collective-permute-done((bf16[256,512]{1,0:T(8,128)(2,1)S(1)}, bf16[256,512]{1,0:T(8,128)(2,1)S(1)}, u32[]{:S(2)}, u32[]{:S(2)}) %collective-permute-start.16) | collective-permute-done | bytes 262176 | tf_op jit(solution)/shard_map/ppermute | solution.py:234
  134.2 5.1 %collective-permute-start.20 = (bf16[256,512]{1,0:T(8,128)(2,1)S(1)}, bf16[256,512]{1,0:T(8,128)(2,1)S(1)}, u32[]{:S(2)}, u32[]{:S(2)}) collective-permute-start(bf16[256,512]{1,0:T(8,128)(2,1)S(1)} %fusion.5), channel_id=1, source_target_pairs={{0,8},{1,24},{2,12},{3,28},{8,9},{9,25},{10,13},{11,29},{16,10},{1... | collective-permute-start | bytes 786440 | tf_op jit(solution)/shard_map/ppermute | solution.py:234
  140.7 5.1 %collective-permute-done.20 = bf16[256,512]{1,0:T(8,128)(2,1)S(1)} collective-permute-done((bf16[256,512]{1,0:T(8,128)(2,1)S(1)}, bf16[256,512]{1,0:T(8,128)(2,1)S(1)}, u32[]{:S(2)}, u32[]{:S(2)}) %collective-permute-start.20) | collective-permute-done | bytes 262176 | tf_op jit(solution)/shard_map/ppermute | solution.py:234
  145.8 6.4 %collective-permute-done.21 = bf16[256,512]{1,0:T(8,128)(2,1)S(1)} collective-permute-done((bf16[256,512]{1,0:T(8,128)(2,1)S(1)}, bf16[256,512]{1,0:T(8,128)(2,1)S(1)}, u32[]{:S(2)}, u32[]{:S(2)}) %collective-permute-start.21) | collective-permute-done | bytes 262176 | tf_op jit(solution)/shard_map/ppermute | solution.py:234
  (73 shorter events, 19.9 us)
Async XLA Ops:
  2.8 40.7 %all-to-all-start = ((bf16[8,3,256,128]{3,2,1,0:T(8,128)(2,1)}), bf16[8,3,256,128]{3,2,1,0:T(8,128)(2,1)S(1)}, u32[]{:S(2)}, u32[]{:S(2)}) async-start(bf16[8,3,256,128]{3,2,1,0:T(8,128)(2,1)} %pack.1), calls=%async_computation | async-start | bytes 3145728 | tf_op jit(solution)/shard_map/all_to_all | solution.py:176
  47.4 47.9 %copy-start.1 = (bf16[1024,128]{1,0:T(8,128)(2,1)}, bf16[1024,128]{1,0:T(8,128)(2,1)S(1)}, u32[]{:S(2)}) copy-start(bf16[1024,128]{1,0:T(8,128)(2,1)S(1)} %get-tuple-element.20.refs_0_) | copy-start | bytes 786436
  47.4 10.0 %collective-permute-start = (bf16[1024,128]{1,0:T(8,128)(2,1)S(1)}, bf16[1024,128]{1,0:T(8,128)(2,1)S(1)}, u32[]{:S(2)}, u32[]{:S(2)}) collective-permute-start(bf16[1024,128]{1,0:T(8,128)(2,1)S(1)} %get-tuple-element.19.refs_0_), channel_id=1, source_target_pairs={{8,16},{16,24},{24,28},{28,20},{20,12},{12,4},{4,0},{0,8},{9,17},{... | collective-permute-start | bytes 786440 | tf_op jit(solution)/shard_map/ppermute | solution.py:199
  48.4 10.1 %collective-permute-start.1 = (bf16[1024,128]{1,0:T(8,128)(2,1)S(1)}, bf16[1024,128]{1,0:T(8,128)(2,1)S(1)}, u32[]{:S(2)}, u32[]{:S(2)}) collective-permute-start(bf16[1024,128]{1,0:T(8,128)(2,1)S(1)} %get-tuple-element.19.refs_0_), channel_id=1, source_target_pairs={{16,8},{24,16},{28,24},{20,28},{12,20},{4,12},{0,4},{8,0},{17,9},{... | collective-permute-start | bytes 786440 | tf_op jit(solution)/shard_map/ppermute | solution.py:199
  50.2 12.8 %collective-permute-start.4 = (bf16[1024,128]{1,0:T(8,128)(2,1)S(1)}, bf16[1024,128]{1,0:T(8,128)(2,1)S(1)}, u32[]{:S(2)}, u32[]{:S(2)}) collective-permute-start(bf16[1024,128]{1,0:T(8,128)(2,1)S(1)} %get-tuple-element.20.refs_0_), channel_id=1, source_target_pairs={{8,16},{16,24},{24,28},{28,20},{20,12},{12,4},{4,0},{0,8},{9,17},{... | collective-permute-start | bytes 786440 | tf_op jit(solution)/shard_map/ppermute | solution.py:199
  51.3 12.8 %collective-permute-start.5 = (bf16[1024,128]{1,0:T(8,128)(2,1)S(1)}, bf16[1024,128]{1,0:T(8,128)(2,1)S(1)}, u32[]{:S(2)}, u32[]{:S(2)}) collective-permute-start(bf16[1024,128]{1,0:T(8,128)(2,1)S(1)} %get-tuple-element.20.refs_0_), channel_id=1, source_target_pairs={{16,8},{24,16},{28,24},{20,28},{12,20},{4,12},{0,4},{8,0},{17,9},{... | collective-permute-start | bytes 786440 | tf_op jit(solution)/shard_map/ppermute | solution.py:199
  57.4 11.2 %collective-permute-start.2 = (bf16[1024,128]{1,0:T(8,128)(2,1)S(1)}, bf16[1024,128]{1,0:T(8,128)(2,1)S(1)}, u32[]{:S(2)}, u32[]{:S(2)}) collective-permute-start(bf16[1024,128]{1,0:T(8,128)(2,1)S(1)} %collective-permute-done.refs_1_), channel_id=1, source_target_pairs={{8,16},{16,24},{24,28},{28,20},{20,12},{12,4},{4,0},{0,8},{9,17},{... | collective-permute-start | bytes 786440 | tf_op jit(solution)/shard_map/ppermute | solution.py:199
  58.4 11.2 %collective-permute-start.3 = (bf16[1024,128]{1,0:T(8,128)(2,1)S(1)}, bf16[1024,128]{1,0:T(8,128)(2,1)S(1)}, u32[]{:S(2)}, u32[]{:S(2)}) collective-permute-start(bf16[1024,128]{1,0:T(8,128)(2,1)S(1)} %collective-permute-done.1.refs_2_), channel_id=1, source_target_pairs={{16,8},{24,16},{28,24},{20,28},{12,20},{4,12},{0,4},{8,0},{17,9},{... | collective-permute-start | bytes 786440 | tf_op jit(solution)/shard_map/ppermute | solution.py:199
  63.0 13.2 %collective-permute-start.8 = (bf16[1024,128]{1,0:T(8,128)(2,1)S(1)}, bf16[1024,128]{1,0:T(8,128)(2,1)S(1)}, u32[]{:S(2)}, u32[]{:S(2)}) collective-permute-start(bf16[1024,128]{1,0:T(8,128)(2,1)S(1)} %collective-permute-done.4.refs_1_), channel_id=1, source_target_pairs={{8,16},{16,24},{24,28},{28,20},{20,12},{12,4},{4,0},{0,8},{9,17},{... | collective-permute-start | bytes 786440 | tf_op jit(solution)/shard_map/ppermute | solution.py:199
  64.1 11.2 %collective-permute-start.9 = (bf16[1024,128]{1,0:T(8,128)(2,1)S(1)}, bf16[1024,128]{1,0:T(8,128)(2,1)S(1)}, u32[]{:S(2)}, u32[]{:S(2)}) collective-permute-start(bf16[1024,128]{1,0:T(8,128)(2,1)S(1)} %collective-permute-done.5.refs_2_), channel_id=1, source_target_pairs={{16,8},{24,16},{28,24},{20,28},{12,20},{4,12},{0,4},{8,0},{17,9},{... | collective-permute-start | bytes 786440 | tf_op jit(solution)/shard_map/ppermute | solution.py:199
  69.7 10.2 %collective-permute-start.6 = (bf16[1024,128]{1,0:T(8,128)(2,1)S(1)}, bf16[1024,128]{1,0:T(8,128)(2,1)S(1)}, u32[]{:S(2)}, u32[]{:S(2)}) collective-permute-start(bf16[1024,128]{1,0:T(8,128)(2,1)S(1)} %collective-permute-done.2.refs_3_), channel_id=1, source_target_pairs={{8,16},{16,24},{24,28},{28,20},{20,12},{12,4},{4,0},{0,8},{9,17},{... | collective-permute-start | bytes 786440 | tf_op jit(solution)/shard_map/ppermute | solution.py:199
  71.7 9.2 %collective-permute-start.7 = (bf16[1024,128]{1,0:T(8,128)(2,1)S(1)}, bf16[1024,128]{1,0:T(8,128)(2,1)S(1)}, u32[]{:S(2)}, u32[]{:S(2)}) collective-permute-start(bf16[1024,128]{1,0:T(8,128)(2,1)S(1)} %collective-permute-done.3.refs_4_), channel_id=1, source_target_pairs={{16,8},{24,16},{28,24},{20,28},{12,20},{4,12},{0,4},{8,0},{17,9},{... | collective-permute-start | bytes 786440 | tf_op jit(solution)/shard_map/ppermute | solution.py:199
  75.3 10.3 %collective-permute-start.12 = (bf16[1024,128]{1,0:T(8,128)(2,1)S(1)}, bf16[1024,128]{1,0:T(8,128)(2,1)S(1)}, u32[]{:S(2)}, u32[]{:S(2)}) collective-permute-start(bf16[1024,128]{1,0:T(8,128)(2,1)S(1)} %collective-permute-done.9.refs_4_), channel_id=1, source_target_pairs={{16,8},{24,16},{28,24},{20,28},{12,20},{4,12},{0,4},{8,0},{17,9},{... | collective-permute-start | bytes 786440 | tf_op jit(solution)/shard_map/ppermute | solution.py:199
  76.3 9.3 %collective-permute-start.11 = (bf16[1024,128]{1,0:T(8,128)(2,1)S(1)}, bf16[1024,128]{1,0:T(8,128)(2,1)S(1)}, u32[]{:S(2)}, u32[]{:S(2)}) collective-permute-start(bf16[1024,128]{1,0:T(8,128)(2,1)S(1)} %collective-permute-done.8.refs_3_), channel_id=1, source_target_pairs={{8,16},{16,24},{24,28},{28,20},{20,12},{12,4},{4,0},{0,8},{9,17},{... | collective-permute-start | bytes 786440 | tf_op jit(solution)/shard_map/ppermute | solution.py:199
  81.7 7.8 %collective-permute-start.10 = (bf16[1024,128]{1,0:T(8,128)(2,1)S(1)}, bf16[1024,128]{1,0:T(8,128)(2,1)}, u32[]{:S(2)}, u32[]{:S(2)}) collective-permute-start(bf16[1024,128]{1,0:T(8,128)(2,1)S(1)} %collective-permute-done.6.refs_5_), channel_id=1, source_target_pairs={{8,16},{16,24},{24,28},{28,20},{20,12},{12,4},{4,0},{0,8},{9,17},{... | collective-permute-start | bytes 786440 | tf_op jit(solution)/shard_map/ppermute | solution.py:199
  95.4 8.8 %collective-permute-start.13 = (bf16[512,512]{1,0:T(8,128)(2,1)}, bf16[512,512]{1,0:T(8,128)(2,1)S(1)}, u32[]{:S(2)}, u32[]{:S(2)}) collective-permute-start(bf16[512,512]{1,0:T(8,128)(2,1)} %get-tuple-element.26), channel_id=1, source_target_pairs={{0,1},{1,0},{2,3},{3,2},{4,5},{5,4},{6,7},{7,6},{8,9},{9,8},{10,11... | collective-permute-start | bytes 1572872 | tf_op jit(solution)/shard_map/ppermute | solution.py:212
  95.5 8.7 %collective-permute-start.14 = (bf16[1024,128]{1,0:T(8,128)(2,1)S(1)}, bf16[1024,128]{1,0:T(8,128)(2,1)S(1)}, u32[]{:S(2)}, u32[]{:S(2)}) collective-permute-start(bf16[1024,128]{1,0:T(8,128)(2,1)S(1)} %collective-permute-done.12.refs_6_), channel_id=1, source_target_pairs={{16,8},{24,16},{28,24},{20,28},{12,20},{4,12},{0,4},{8,0},{17,9},{... | collective-permute-start | bytes 786440 | tf_op jit(solution)/shard_map/ppermute | solution.py:199
  111.3 13.3 %collective-permute-start.17 = (bf16[512,512]{1,0:T(8,128)(2,1)}, bf16[512,512]{1,0:T(8,128)(2,1)S(1)}, u32[]{:S(2)}, u32[]{:S(2)}) collective-permute-start(bf16[512,512]{1,0:T(8,128)(2,1)} %get-tuple-element.30), channel_id=1, source_target_pairs={{0,1},{1,0},{2,3},{3,2},{4,5},{5,4},{6,7},{7,6},{8,9},{9,8},{10,11... | collective-permute-start | bytes 1572872 | tf_op jit(solution)/shard_map/ppermute | solution.py:212
  111.4 8.7 %collective-permute-start.15 = (bf16[1,256,512]{2,1,0:T(8,128)(2,1)S(1)}, bf16[1,256,512]{2,1,0:T(8,128)(2,1)S(1)}, u32[]{:S(2)}, u32[]{:S(2)}) collective-permute-start(bf16[1,256,512]{2,1,0:T(8,128)(2,1)S(1)} %fusion.2), channel_id=1, source_target_pairs={{0,2},{1,3},{2,0},{3,1},{4,6},{5,7},{6,4},{7,5},{8,10},{9,11},{10,... | collective-permute-start | bytes 786440 | tf_op jit(solution)/shard_map/ppermute | solution.py:222
  120.2 13.3 %collective-permute-start.16 = (bf16[256,512]{1,0:T(8,128)(2,1)S(1)}, bf16[256,512]{1,0:T(8,128)(2,1)S(1)}, u32[]{:S(2)}, u32[]{:S(2)}) collective-permute-start(bf16[256,512]{1,0:T(8,128)(2,1)S(1)} %fusion.4), channel_id=1, source_target_pairs={{0,0},{1,16},{2,4},{3,20},{8,1},{9,17},{10,5},{11,21},{16,2},{17,1... | collective-permute-start | bytes 786440 | tf_op jit(solution)/shard_map/ppermute | solution.py:234
  124.0 9.6 %collective-permute-start.19 = (bf16[256,512]{1,0:T(8,128)(2,1)S(1)}, bf16[256,512]{1,0:T(8,128)(2,1)S(1)}, u32[]{:S(2)}, u32[]{:S(2)}) collective-permute-start(bf16[256,512]{1,0:T(8,128)(2,1)S(1)} %fusion.4), channel_id=1, source_target_pairs={{4,0},{5,16},{6,4},{7,20},{12,1},{13,17},{14,5},{15,21},{20,2},{21... | collective-permute-start | bytes 786440 | tf_op jit(solution)/shard_map/ppermute | solution.py:234
  125.9 8.2 %collective-permute-start.18 = (bf16[1,256,512]{2,1,0:T(8,128)(2,1)S(1)}, bf16[1,256,512]{2,1,0:T(8,128)(2,1)S(1)}, u32[]{:S(2)}, u32[]{:S(2)}) collective-permute-start(bf16[1,256,512]{2,1,0:T(8,128)(2,1)S(1)} %fusion.3), channel_id=1, source_target_pairs={{0,2},{1,3},{2,0},{3,1},{4,6},{5,7},{6,4},{7,5},{8,10},{9,11},{10,... | collective-permute-start | bytes 786440 | tf_op jit(solution)/shard_map/ppermute | solution.py:222
  134.2 11.6 %collective-permute-start.20 = (bf16[256,512]{1,0:T(8,128)(2,1)S(1)}, bf16[256,512]{1,0:T(8,128)(2,1)S(1)}, u32[]{:S(2)}, u32[]{:S(2)}) collective-permute-start(bf16[256,512]{1,0:T(8,128)(2,1)S(1)} %fusion.5), channel_id=1, source_target_pairs={{0,8},{1,24},{2,12},{3,28},{8,9},{9,25},{10,13},{11,29},{16,10},{1... | collective-permute-start | bytes 786440 | tf_op jit(solution)/shard_map/ppermute | solution.py:234
  139.3 12.9 %collective-permute-start.21 = (bf16[256,512]{1,0:T(8,128)(2,1)S(1)}, bf16[256,512]{1,0:T(8,128)(2,1)S(1)}, u32[]{:S(2)}, u32[]{:S(2)}) collective-permute-start(bf16[256,512]{1,0:T(8,128)(2,1)S(1)} %fusion.5), channel_id=1, source_target_pairs={{4,8},{5,24},{6,12},{7,28},{12,9},{13,25},{14,13},{15,29},{20,10},... | collective-permute-start | bytes 786440 | tf_op jit(solution)/shard_map/ppermute | solution.py:234
  (17 other events, 370.8 us)
